TPU v7x, 256 devices: a whole 4x4x8 slice. The times are simulated.
256 devices in a mesh: dp: 32 (over x, z), mp: 8 (over y, core).
Axes of the slice: x: 4, y: 4, z: 8, core: 2. Of those that a mesh axis runs over, the one named last changes fastest.
Arguments:
- teacher_feat: bfloat16 [3072, 256], P('dp'), may hold values from -6 to 6
- student_feat: bfloat16 [15360, 256], P('dp'), may hold values from -6 to 6
- teacher_weight: bfloat16 [256, 65536], P(None, 'mp'), may hold values from -1.5 to 1.5
- student_weight: bfloat16 [256, 65536], P(None, 'mp'), may hold values from -0.375 to 0.375
- crop_to_image: int32 [15360], P('dp'), may hold values from 0 to 95
Outputs:
- feat_grad: float32 [15360, 256], P('dp', 'mp')
- proto_grad: float32 [256, 65536], P('dp', 'mp')
Inputs may be any that keep to these rules, and one draw needn't show every extreme that they name: `crop_to_image`: crop c of the data block d names teacher row d * 96 + crop_to_image_c.
All inputs are finite; a program needn't handle non-finite values.
Results may differ from a plain program's by a relative error of at most 0.0015.
The roundings to bfloat16 on the way count: a program that leaves them out, or rounds other values in their place, can miss the bound.
Values sent between devices are 32-bit elements; how exact they have to be, the bound alone decides.
No kernel may reach another device: no remote copies, remote signals or barrier semaphores. Data moves between devices by JAX's collectives and lax.ppermute only.
A program may use at most 128 MiB of HBM per device.

v0:
```python
import functools

import jax
import jax.numpy as jnp
from jax import lax
from jax.experimental import pallas as pl
from jax.experimental.pallas import tpu as pltpu
from jax.sharding import Mesh
from jax.sharding import PartitionSpec as P

K = 256
P_SIZE = 65536
TB_DEV = 96
TB_TOTAL = 3072
ITERS = 3
SB_DEV = 480
NX, NZ, NY, NC = 4, 8, 4, 2
NROW = NX * NY * NC
COLS = P_SIZE // NROW
LG = COLS // 128
TROWS = NX * TB_DEV
SROWS = NX * SB_DEV

eps = 1e-06
t_temp = 0.07
s_temp = 0.1
loss_scale = 1024.0

f32 = jnp.float32
bf16 = jnp.bfloat16
MIB = 1024 * 1024
GRAD_MIB = 28
LOG2E = 1.4426950408889634
HALF = COLS // 2


def unit_scale(v):
    return lax.rsqrt(jnp.sum(v * v, axis=1, keepdims=True) + eps)


def norm_columns(w):
    v = w.astype(f32)
    return (v * lax.rsqrt(jnp.sum(v * v, axis=0, keepdims=True) + eps)).astype(bf16)


def dot(a, b, ca, cb):
    return lax.dot_general(a, b, (((ca,), (cb,)), ((), ())), preferred_element_type=f32)


def lane_groups(v):
    return jnp.concatenate([v[:, 128 * k : 128 * (k + 1)] for k in range(v.shape[1] // 128)], 0)


def in_hbm(v):
    return pltpu.with_memory_space_constraint(v, pltpu.HBM)


def in_vmem(v):
    return pltpu.with_memory_space_constraint(v, pltpu.VMEM)


def cost(us):
    return pl.CostEstimate(flops=int(us * 1e9), bytes_accessed=0, transcendentals=0)


def call(kernel, out_shape, name, mib, scratch=(), us=1):
    return pl.pallas_call(
        kernel,
        out_shape=out_shape,
        cost_estimate=cost(us),
        scratch_shapes=list(scratch),
        compiler_params=pltpu.CompilerParams(vmem_limit_bytes=mib * MIB),
        name=name,
    )


def arr(*shape, dtype=f32):
    return jax.ShapeDtypeStruct(shape, dtype)


def norm_kernel(at, w, *outs):
    n = norm_columns(w[...])
    for out in outs:
        out[...] = n


def norm_pass(at, w, outs, name):
    return pl.pallas_call(
        norm_kernel,
        grid_spec=pltpu.PrefetchScalarGridSpec(
            num_scalar_prefetch=1,
            grid=(2,),
            in_specs=[pl.BlockSpec((K, 1024), lambda j, at: (0, at[0] * 2 + j))],
            out_specs=[pl.BlockSpec((K, 1024), lambda j, at: (0, j))] * len(outs),
        ),
        out_shape=outs,
        cost_estimate=cost(2),
        compiler_params=pltpu.CompilerParams(vmem_limit_bytes=12 * MIB),
        name=name,
    )(at, in_hbm(w))


def pack_kernel(at, sf, crops, own, half):
    n = SB_DEV // NC
    own[:SB_DEV, :] = sf[...].astype(f32)
    own[SB_DEV:, :] = crops[...]
    half[:n, :] = own[pl.ds(pl.multiple_of(at[1] * n, 8), n), :]
    row = jnp.where(at[1] == 0, crops[0:1, :], crops[1:2, :])
    half[n:, :] = jnp.broadcast_to(row, (8, K))


def pack_pass(at, sf, crops):
    outs = [pltpu.HBM((SB_DEV + 8, K), f32), pltpu.HBM((SB_DEV // NC + 8, K), f32)]
    return small_call(pack_kernel, outs, "pack_rows", at, sf, crops)


def exponentials(tu, tn, j):
    return jnp.exp2(dot(tu[...], tn[:, 512 * j : 512 * (j + 1)], 1, 0) * (LOG2E / t_temp))


def put_columns(c_out, j, c):
    for k in range(4):
        part = c[None, :, 128 * k : 128 * (k + 1)]
        c_out[:, 4 * j + k : 4 * j + k + 1, :] = jnp.broadcast_to(part, (NZ, 1, 128))


def teacher_kernel(tf, tn, c_out, tu_out):
    for x in range(NX):
        v = tf[x]
        tu_out[x * TB_DEV : (x + 1) * TB_DEV, :] = (v * unit_scale(v)).astype(bf16)
    for j in range(COLS // 512):
        put_columns(c_out, j, jnp.sum(exponentials(tu_out, tn, j), axis=0, keepdims=True))


def teacher_pass(tf_all, tn):
    outs = [arr(NZ, LG, 128), pltpu.VMEM((TROWS, K), bf16)]
    return call(teacher_kernel, outs, "teacher_scores", 12)(tf_all, in_vmem(tn))


def row_kernel(tail, c_parts, tu, tn, *refs):
    if tail:
        extra, b_out, r_out = refs
        r_out[:, 8:, :] = jnp.broadcast_to(extra[...][None], (NROW, 16, 128))
    else:
        (r_out,) = refs
    b = 1.0 / (jnp.sum(c_parts[...], axis=0) * P_SIZE)
    if tail:
        b_out[...] = b
    acc = None
    for j in range(COLS // 512):
        e = exponentials(tu, tn, j)
        for k in range(4):
            part = e[:, 128 * k : 128 * (k + 1)] * b[4 * j + k : 4 * j + k + 1, :]
            acc = part if acc is None else acc + part
    r = [jnp.sum(acc[128 * k : 128 * (k + 1), :].T, axis=0, keepdims=True) for k in range(3)]
    r = jnp.concatenate(r + [jnp.ones((5, 128), f32)], 0)
    r_out[:, :8, :] = jnp.broadcast_to(r[None], (NROW, 8, 128))


def row_pass(c_parts, tu, tn, *extra):
    tail = len(extra) > 0
    outs = [arr(LG, 128), arr(NROW, 24, 128)] if tail else [arr(NROW, 8, 128)]
    name = "last_row_sums" if tail else "row_sums"
    kernel = functools.partial(row_kernel, tail)
    return call(kernel, outs, name, 12)(c_parts, in_vmem(tu), in_vmem(tn), *extra)


def col_kernel(r_parts, tu, tn, c_out):
    a = 1.0 / (jnp.sum(r_parts[...], axis=0) * TB_TOTAL)
    wide = jnp.concatenate([jnp.broadcast_to(a[k : k + 1, :], (128, 128)).T for k in range(3)], 0)
    wide = jnp.concatenate([wide] * 4, 1)
    for j in range(COLS // 512):
        put_columns(c_out, j, jnp.sum(exponentials(tu, tn, j) * wide, axis=0, keepdims=True))


def col_pass(r_parts, tu, tn):
    return call(col_kernel, arr(NZ, LG, 128), "col_sums", 12)(r_parts, in_vmem(tu), in_vmem(tn))


def rows_kernel(at, own, mine_1, mine_2, mine_3, core_1, core_2, core_3, tu, *refs):
    ub_out, ubt_out, ut_out, tuc_out, crop_out, mine_out, sf = refs
    ix, ic = at[0], at[1]
    half = SB_DEV // NC
    spare = jnp.zeros((1, 512 - SB_DEV), f32)
    crop_out[...] = jnp.zeros_like(crop_out)
    sf[ix] = own[:SB_DEV, :]
    row = jnp.concatenate([own[SB_DEV : SB_DEV + 1, :half], own[SB_DEV + 1 : SB_DEV + 2, :half], spare], 1)
    crop_out[ix, 0:1, :] = row
    for d, mine, core in ((1, mine_1, core_1), (2, mine_2, core_2), (3, mine_3, core_3)):
        x = lax.rem(ix + NX - d, NX)
        sf[x, pl.ds(pl.multiple_of(ic * half, 8), half), :] = mine[:half, :]
        sf[x, pl.ds(pl.multiple_of((1 - ic) * half, 8), half), :] = core[:half, :]
        m, c = mine[half : half + 1, :half], core[half : half + 1, :half]
        row = jnp.concatenate([jnp.where(ic == 0, m, c), jnp.where(ic == 0, c, m), spare], 1)
        crop_out[x, 0:1, :] = row
    for x in range(NX):
        rows = slice(x * SB_DEV, (x + 1) * SB_DEV)
        v = sf[x]
        scale = unit_scale(v)
        u = v * scale
        ub_out[rows, :] = u.astype(bf16)
        crop_out[x, 1:2, :SB_DEV] = jnp.broadcast_to(scale, (SB_DEV, 128)).T[0:1, :]
        ut = u.T
        ut_out[x] = ut
        ubt_out[x] = ut.astype(bf16)
        row = lax.broadcasted_iota(jnp.int32, (TB_DEV, SB_DEV), 0)
        pick = row == crop_out[x, 0:1, :SB_DEV].astype(jnp.int32)
        pick = jnp.where(pick, 1.0, 0.0).astype(bf16)
        tuc_out[rows, :] = dot(pick, tu[x * TB_DEV : (x + 1) * TB_DEV, :], 0, 0).astype(bf16)
    mine_out[:32, :] = ut_out[ix, pl.ds(pl.multiple_of((at[3] * NC + ic) * 32, 8), 32), :]
    mine_out[32:, :] = jnp.broadcast_to(crop_out[ix, 1:2, :SB_DEV], (8, SB_DEV))


def rows_pass(at, own, mine, core, tu):
    whole = lambda shape: pl.BlockSpec(shape, lambda i, at: (0,) * len(shape))
    half = whole((SB_DEV // NC + 8, K))
    outs = [
        arr(SROWS, K, dtype=bf16),
        arr(NX, K, SB_DEV, dtype=bf16),
        arr(NX, K, SB_DEV),
        arr(SROWS, K, dtype=bf16),
        arr(NX, 8, 512),
        arr(40, SB_DEV),
    ]
    return pl.pallas_call(
        rows_kernel,
        grid_spec=pltpu.PrefetchScalarGridSpec(
            num_scalar_prefetch=1,
            grid=(1,),
            in_specs=[whole((SB_DEV + 8, K))] + [half] * 6 + [whole((TROWS, K))],
            out_specs=[whole(v.shape) for v in outs],
            scratch_shapes=[pltpu.VMEM((NX, SB_DEV, K), f32)],
        ),
        out_shape=[pltpu.HBM(v.shape, v.dtype) for v in outs],
        cost_estimate=cost(3),
        compiler_params=pltpu.CompilerParams(vmem_limit_bytes=20 * MIB),
        name="student_units",
    )(at, *[in_hbm(v) for v in (own, *mine, *core)], tu)


def student_kernel(ub, sn, rs_out):
    @pl.loop(0, NX)
    def _(x):
        rows = pl.ds(pl.multiple_of(x * SB_DEV, 32), SB_DEV)
        total = None
        for j in range(COLS // 512):
            e = jnp.exp2(dot(ub[rows, :], sn[:, 512 * j : 512 * (j + 1)], 1, 0) * (LOG2E / s_temp))
            for k in range(4):
                part = e[:, 128 * k : 128 * (k + 1)]
                total = part if total is None else total + part
        for k in range(4):
            part = total[128 * k : min(128 * (k + 1), SB_DEV), :].T
            part = jnp.sum(part, axis=0, keepdims=True)
            if part.shape[1] < 128:
                part = jnp.concatenate([part, jnp.ones((1, 128 - part.shape[1]), f32)], 1)
            rs_out[pl.ds(4 * x + k, 1), :] = part


def student_pass(ub, sn):
    return call(student_kernel, arr(16, 128), "student_sums", 14, us=3)(ub, sn)


def factors(crops, parts, coef):
    total = jnp.sum(parts[...], axis=0)
    a = (loss_scale / s_temp) / total[:3]
    a = jnp.concatenate([a[0:1], a[1:2], a[2:3]], 1)
    s = (loss_scale / s_temp) / total[8:]
    row = lax.broadcasted_iota(jnp.int32, (TB_DEV, SB_DEV), 0)
    lane = lax.broadcasted_iota(jnp.int32, (128, 128), 1)
    for x in range(NX):
        ax = jnp.concatenate([a[:, x * TB_DEV : (x + 1) * TB_DEV], jnp.zeros((1, 32), f32)], 1)
        ax = jnp.broadcast_to(ax, (128, 128)).T[:TB_DEV, 0:1]
        pick = row == crops[x, 0:1, :SB_DEV].astype(jnp.int32)
        ac = jnp.sum(jnp.where(pick, ax, 0.0), axis=0, keepdims=True)
        ac = jnp.concatenate([ac, jnp.zeros((1, 512 - SB_DEV), f32)], 1)
        for k in range(4):
            ak = jnp.broadcast_to(ac[:, 128 * k : 128 * (k + 1)], (128, 128)).T
            sk = jnp.broadcast_to(s[4 * x + k : 4 * x + k + 1, :], (128, 128)).T
            n = min(128, SB_DEV - 128 * k)
            both = jnp.where(lane == 0, ak, sk)
            coef[x * SB_DEV + 128 * k : x * SB_DEV + 128 * k + n, :] = both[:n]


def grad_half(h, iz, ub, ubt, tuc, coef, b, sn, tn, p, p_outs, take):
    cols = slice(h * HALF, (h + 1) * HALF)
    bh = jnp.concatenate([b[k : k + 1, :] for k in range(h * LG // 2, (h + 1) * LG // 2)], 1)
    for x in range(NX):
        rows = slice(x * SB_DEV, (x + 1) * SB_DEV)
        q = jnp.exp2(dot(ub[rows, :], sn[:, cols], 1, 0) * (LOG2E / s_temp)) * coef[rows, 1:2]
        t = jnp.exp2(dot(tuc[rows, :], tn[:, cols], 1, 0) * (LOG2E / t_temp)) * bh
        d = (q - t * coef[rows, 0:1]).astype(bf16)
        prod = dot(ubt[x], d, 1, 0)
        if x == 0:
            p[...] = prod
        else:
            p[...] += prod
        take(x, rows, dot(d, sn[:, cols], 1, 1))
    for d in range(NZ):
        z = lax.rem(iz + d, NZ)
        for x in range(NX):
            p_outs[d][x] = p[pl.ds(pl.multiple_of(x * 64 + z * 8, 8), 8), :]


def first_kernel(at, crops, parts, ub, ubt, tuc, b, sn, tn, *refs):
    *p_outs, g_out, coef, p = refs
    factors(crops, parts, coef)

    def take(x, rows, part):
        g_out[rows, :] = part

    grad_half(0, at[2], ub, ubt, tuc, coef, b, sn, tn, p, p_outs, take)


def second_kernel(at, coef, g_in, ut, ub, ubt, tuc, b, sn, tn, *refs):
    *p_outs, g_out, p, g, sems = refs
    n, spare = NY * NC, SB_DEV // 32
    out = lambda x: pltpu.make_async_copy(g.at[x], g_out.at[pl.ds(x * n, n)], sems.at[x])

    def take(x, rows, part):
        gt = (g_in[rows, :] + part).T
        along = jnp.sum(ut[x] * gt, axis=0, keepdims=True)
        along = [along[:, 32 * i : 32 * (i + 1)] for i in range(spare)]
        along = jnp.concatenate(along + [jnp.zeros((32 - spare, 32), f32)], 0)
        for m in range(n):
            g[x, m] = jnp.concatenate([gt[32 * m : 32 * (m + 1), :], along], 1)
        out(x).start()

    grad_half(1, at[2], ub, ubt, tuc, coef, b, sn, tn, p, p_outs, take)
    for x in range(NX):
        out(x).wait()


def grad_call(kernel, outs, specs, name, scratch, at, *args):
    whole = lambda v: pl.BlockSpec(v.shape, lambda i, at, n=len(v.shape): (0,) * n)
    return pl.pallas_call(
        kernel,
        grid_spec=pltpu.PrefetchScalarGridSpec(
            num_scalar_prefetch=1,
            grid=(1,),
            in_specs=[whole(v) for v in args],
            out_specs=[whole(arr(NX, 8, HALF))] * NZ + (specs or [whole(v) for v in outs]),
            scratch_shapes=[pltpu.VMEM((K, HALF), f32)] + scratch,
        ),
        out_shape=[pltpu.HBM((NX, 8, HALF), f32)] * NZ + outs,
        cost_estimate=cost(8),
        compiler_params=pltpu.CompilerParams(vmem_limit_bytes=GRAD_MIB * MIB),
        name=name,
    )(at, *args)


def first_pass(at, crops, parts, *common):
    outs = [arr(SROWS, K), arr(SROWS, 128)]
    *p, g, coef = grad_call(first_kernel, outs, None, "first_half", [], at, crops, parts, *common)
    return p, g, coef


def second_pass(at, coef, g, ut, *common):
    outs, specs = [pltpu.HBM((NROW, 32, 512), f32)], [pl.BlockSpec(memory_space=pltpu.HBM)]
    scratch = [pltpu.VMEM((NX, NY * NC, 32, 512), f32), pltpu.SemaphoreType.DMA((NX,))]
    *p, g = grad_call(second_kernel, outs, specs, "second_half", scratch, at, coef, g, ut, *common)
    return p, g


def feat_kernel(parts, mine, out):
    g = jnp.sum(parts[...], axis=0)
    along = jnp.concatenate([g[i : i + 1, SB_DEV:] for i in range(SB_DEV // 32)], 1)
    out[...] = (g[:, :SB_DEV] - mine[:32, :] * along) * mine[32:33, :]


def feat_pass(parts, mine):
    return call(feat_kernel, arr(32, SB_DEV), "feat_grad", 8)(parts, mine)


def merge_kernel(at, p0, u0, d0, p1, u1, d1, *outs):
    for d in range(NX):
        x = lax.rem(at[0] + d, NX)
        outs[d][:, :HALF] = p0[x] + u0[x] + d0[x]
        outs[d][:, HALF:] = p1[x] + u1[x] + d1[x]


def merge_pass(at, *args):
    return small_call(merge_kernel, [arr(8, COLS)] * NX, "merge_sums", at, *args)


def proto_kernel(at, *refs):
    out = refs[NX]
    for d in range(NX):
        x = lax.rem(at[0] + NX - d, NX)
        out[:, pl.ds(pl.multiple_of(x * COLS, 128), COLS)] = refs[d][...]


def proto_pass(at, *args):
    return small_call(proto_kernel, [arr(8, NX * COLS)], "proto_grad", at, *args)[0]


def small_call(kernel, outs, name, at, *args):
    whole = lambda v: pl.BlockSpec(v.shape, lambda i, at, n=len(v.shape): (0,) * n)
    return pl.pallas_call(
        kernel,
        grid_spec=pltpu.PrefetchScalarGridSpec(
            num_scalar_prefetch=1,
            grid=(1,),
            in_specs=[whole(v) for v in args],
            out_specs=[whole(v) for v in outs],
        ),
        out_shape=outs,
        cost_estimate=cost(1),
        compiler_params=pltpu.CompilerParams(vmem_limit_bytes=6 * MIB),
        name=name,
    )(at, *args)


def shift(v, axis, size, d):
    return lax.ppermute(v, axis, [(i, (i + d) % size) for i in range(size)])


def exchange(v, axes):
    return lax.all_to_all(v, axes, 0, 0, tiled=False)


def shards(teacher_feat, student_feat, teacher_weight, student_weight, crop_to_image):
    ix, iz = lax.axis_index("x"), lax.axis_index("z")
    iy, ic = lax.axis_index("y"), lax.axis_index("c")
    at = jnp.stack([ix, ic, iz, iy]).astype(jnp.int32)
    group = ("x", "y", "c")
    together = lax.optimization_barrier

    tf_all = jnp.broadcast_to(teacher_feat.astype(f32)[None], (NX, TB_DEV, K))
    tf_all = exchange(tf_all, ("x",))
    rows = SB_DEV // NC
    crops = jnp.pad(crop_to_image.astype(f32).reshape(NC, rows), ((0, 6), (0, K - rows)))
    own, half = pack_pass(at, student_feat, crops)
    mine = [shift(half, "x", NX, d) for d in (1, 3, 2)]
    share = (K, COLS)
    tn, tv = norm_pass(
        at, teacher_weight, [pltpu.HBM(share, bf16), pltpu.VMEM(share, bf16)], "teacher_norm"
    )
    tf_all, tn, tv, own = together((tf_all, tn, tv, own))

    c_parts, tu = teacher_pass(tf_all, tv)
    r_parts = row_pass(exchange(c_parts, ("z",)), tu, tv)[0]
    r_parts, at_1 = together((r_parts, at))
    r_parts = exchange(r_parts, group)
    (sn,) = norm_pass(at_1, student_weight, [pltpu.HBM(share, bf16)], "student_norm")
    c_parts, sn, *mine = together((col_pass(r_parts, tu, tv), sn, *mine))
    c_parts = exchange(c_parts, ("z",))
    core = [shift(v, "c", NC, 1) for v in mine]
    c_parts, *core = together((c_parts, *core))
    r_parts, tu = together((row_pass(c_parts, tu, tv)[0], tu))
    r_parts = exchange(r_parts, group)
    mine, core = (mine[0], mine[2], mine[1]), (core[0], core[2], core[1])
    ub, ubt, ut, tuc, crops, mine = rows_pass(at, own, mine, core, tu)
    r_parts, ub, ubt, ut, tuc = together((r_parts, ub, ubt, ut, tuc))
    c_parts, ub = together((col_pass(r_parts, tu, tv), ub))
    c_parts = exchange(c_parts, ("z",))
    sums = student_pass(ub, sn)
    b, parts = row_pass(c_parts, tu, tv, sums)
    parts = exchange(parts, group)

    common = (ub, ubt, tuc, b, sn, tn)
    p0, g, coef = first_pass(at, crops, parts, *common)
    up = lambda v: shift(v, "z", NZ, 1)
    down = lambda v: shift(v, "z", NZ, -1)
    u0, d0 = up(p0[4]), down(p0[5])
    p1, g = second_pass(at, coef, g, ut, *common)
    u0, d0, g, *p1 = together((u0, d0, g, *p1))
    g = exchange(g, group)
    u1, d1 = up(p1[3]), down(p1[4])
    for k in (3, 2):
        u0, d0 = up(u0 + p0[k]), down(d0 + p0[9 - k])
        u1, d1 = up(u1 + p1[k - 1]), down(d1 + p1[8 - k])
    u0, d1 = up(u0 + p0[1]), down(d1 + p1[7])
    own, *give = merge_pass(at, p0[0], u0, d0, p1[0], u1, d1)
    got = [shift(v, "x", NX, d) for v, d in zip(give, (1, 2, 3))]
    proto_grad = proto_pass(at, own, *got)
    feat_grad = feat_pass(g, mine).T
    return (feat_grad, proto_grad)


def solution(mesh):
    split = Mesh(mesh.devices.reshape(NX, NZ, NY, NC), ("x", "z", "y", "c"))
    dp, mp = ("x", "z"), ("y", "c")
    return jax.shard_map(
        shards,
        mesh=split,
        in_specs=(P(dp, None), P(dp, None), P(None, mp), P(None, mp), P(dp)),
        out_specs=(P(dp, mp), P(dp, mp)),
        check_vma=False,
    )
```

profile of v0, /device:TPU:8, one launch (start us, length us, event | category | flops | bytes accessed | tf_op | source)
XLA Modules:
  0.0 161.5 jit_solution(15326945344279039826)
XLA Ops:
  0.6 1.6 broadcast_in_dim.2
  2.2 4.3 %all-to-all-start = ((f32[4,96,256]{2,1,0:T(8,128)}), f32[4,96,256]{2,1,0:T(8,128)S(1)}, u32[]{:S(2)}, u32[]{:S(2)}) async-start(f32[4,96,256]{2,1,0:T(8,128)} %broadcast_in_dim.2), calls=%async_computation | async-start | bytes 786432 | tf_op jit(solution)/shard_map/all_to_all | solution.py:418
  7.4 0.9 copy-done
  8.3 1.4 pack_rows.1
  9.7 3.0 %teacher_norm.1 = (bf16[256,2048]{1,0:T(8,128)(2,1)}, bf16[256,2048]{1,0:T(8,128)(2,1)S(1)}) custom-call(s32[4]{0:T(128)S(1)} %pad_add_fusion.at, bf16[256,8192]{1,0:T(8,128)(2,1)} %w.2), custom_call_target="tpu_custom_call" | custom-call | flops 2000000000 | tf_op jit(solution)/shard_map/teacher_norm/pallas_call | solution.py:88
  12.8 1.8 %all-to-all-done.tf = f32[4,96,256]{2,1,0:T(8,128)S(1)} async-done(((f32[4,96,256]{2,1,0:T(8,128)}), f32[4,96,256]{2,1,0:T(8,128)S(1)}, u32[]{:S(2)}, u32[]{:S(2)}) %all-to-all-start) | async-done | bytes 393248 | tf_op jit(solution)/shard_map/all_to_all | solution.py:418
  14.6 1.3 teacher_scores.1
  15.9 8.5 %all-to-all-start.1 = ((f32[8,16,128]{2,1,0:T(8,128)}), f32[8,16,128]{2,1,0:T(8,128)S(1)}, u32[]{:S(2)}, u32[]{:S(2)}) async-start(f32[8,16,128]{2,1,0:T(8,128)} %get-tuple-element.80), calls=%async_computation.1 | async-start | bytes 131072 | tf_op jit(solution)/shard_map/all_to_all | solution.py:418
  24.3 1.8 %collective-permute-start.2 = (f32[248,256]{1,0:T(8,128)S(1)}, f32[248,256]{1,0:T(8,128)S(1)}, u32[]{:S(2)}, u32[]{:S(2)}) collective-permute-start(f32[248,256]{1,0:T(8,128)S(1)} %copy-done.25), channel_id=1, source_target_pairs={{0,128},{64,192},{128,0},{192,64},{1,129},{65,193},{129,1},{193,65... | collective-permute-start | bytes 761864 | tf_op jit(solution)/shard_map/ppermute | solution.py:414
  26.1 1.5 collective-permute-start.1
  28.2 4.6 %all-to-all-done.1.c_parts = f32[8,16,128]{2,1,0:T(8,128)S(1)} async-done(((f32[8,16,128]{2,1,0:T(8,128)}), f32[8,16,128]{2,1,0:T(8,128)S(1)}, u32[]{:S(2)}, u32[]{:S(2)}) %all-to-all-start.1) | async-done | bytes 65568 | tf_op jit(solution)/shard_map/all_to_all | solution.py:418
  32.7 1.4 row_sums.2
  34.1 6.2 %all-to-all-start.2 = ((f32[32,8,128]{2,1,0:T(8,128)}), f32[32,8,128]{2,1,0:T(8,128)S(1)}, u32[]{:S(2)}, u32[]{:S(2)}) async-start(f32[32,8,128]{2,1,0:T(8,128)} %row_sums.2), calls=%async_computation.2 | async-start | bytes 262144 | tf_op jit(solution)/shard_map/all_to_all | solution.py:418
  40.3 2.8 %student_norm.1.sn = bf16[256,2048]{1,0:T(8,128)(2,1)} custom-call(s32[4]{0:T(128)S(1)} %pad_add_fusion.at, bf16[256,8192]{1,0:T(8,128)(2,1)} %w.3), custom_call_target="tpu_custom_call" | custom-call | flops 2000000000 | tf_op jit(solution)/shard_map/student_norm/pallas_call | solution.py:88
  43.1 3.8 %all-to-all-done.2.r_parts = f32[32,8,128]{2,1,0:T(8,128)S(1)} async-done(((f32[32,8,128]{2,1,0:T(8,128)}), f32[32,8,128]{2,1,0:T(8,128)S(1)}, u32[]{:S(2)}, u32[]{:S(2)}) %all-to-all-start.2) | async-done | bytes 131104 | tf_op jit(solution)/shard_map/all_to_all | solution.py:418
  48.4 11.8 %all_to_all.40.c_parts = f32[8,16,128]{2,1,0:T(8,128)S(1)} all-to-all(f32[8,16,128]{2,1,0:T(8,128)S(1)} %col_sums.2), channel_id=1, replica_groups=mesh['x'=4,'z'=8,'y'=4,'c'=2] {'z'}, dimensions={0} | all-to-all | bytes 131072 | tf_op jit(solution)/shard_map/all_to_all | solution.py:418
  60.2 1.4 row_sums.3
  61.6 5.0 %all-to-all-start.4 = ((f32[32,8,128]{2,1,0:T(8,128)}), f32[32,8,128]{2,1,0:T(8,128)S(1)}, u32[]{:S(2)}, u32[]{:S(2)}) async-start(f32[32,8,128]{2,1,0:T(8,128)} %row_sums.3), calls=%async_computation.4 | async-start | bytes 262144 | tf_op jit(solution)/shard_map/all_to_all | solution.py:418
  66.6 5.9 %student_units.1 = (bf16[1920,256]{1,0:T(8,128)(2,1)}, bf16[4,256,480]{2,1,0:T(8,128)(2,1)}, f32[4,256,480]{2,1,0:T(8,128)}, bf16[1920,256]{1,0:T(8,128)(2,1)}, f32[4,8,512]{2,1,0:T(8,128)}, /*index=5*/f32[40,480]{1,0:T(8,128)}) custom-call(s32[4]{0:T(128)S(1)} %pad_add_fusion.at, f32[488,256]{1,0:T(8,128)} %get-tuple-element.77.own, f32[248,256]{1,0:T(8,128)} %copy-done.24, ...), custom_call_target="tpu_custom_call" | custom-call | flops 3000000000 | tf_op jit(solution)/shard_map/student_units/pallas_call | solution.py:225
  72.5 0.8 all-to-all-done.4.r_parts
  73.3 1.3 col_sums.3
  74.6 3.4 %all-to-all-start.5 = ((f32[8,16,128]{2,1,0:T(8,128)}), f32[8,16,128]{2,1,0:T(8,128)S(1)}, u32[]{:S(2)}, u32[]{:S(2)}) async-start(f32[8,16,128]{2,1,0:T(8,128)} %col_sums.3), calls=%async_computation.5 | async-start | bytes 131072 | tf_op jit(solution)/shard_map/all_to_all | solution.py:418
  78.0 1.2 copy-done.8
  79.1 3.1 %student_sums.1.refs_0_ = f32[16,128]{1,0:T(8,128)S(1)} custom-call(bf16[1920,256]{1,0:T(8,128)(2,1)S(1)} %copy-done.8, bf16[256,2048]{1,0:T(8,128)(2,1)S(1)} %copy-done.1), custom_call_target="tpu_custom_call" | custom-call | flops 3000000000 | tf_op jit(solution)/shard_map/student_sums/pallas_call | solution.py:260
  82.3 4.0 %all-to-all-done.5.c_parts = f32[8,16,128]{2,1,0:T(8,128)S(1)} async-done(((f32[8,16,128]{2,1,0:T(8,128)}), f32[8,16,128]{2,1,0:T(8,128)S(1)}, u32[]{:S(2)}, u32[]{:S(2)}) %all-to-all-start.5) | async-done | bytes 65568 | tf_op jit(solution)/shard_map/all_to_all | solution.py:418
  87.0 15.5 %all_to_all.41.parts = f32[32,24,128]{2,1,0:T(8,128)S(1)} all-to-all(f32[32,24,128]{2,1,0:T(8,128)S(1)} %get-tuple-element.105), channel_id=1, replica_groups=mesh['x'=4,'z'=8,'y'=4,'c'=2] {'x','y','c'}, dimensions={0} | all-to-all | bytes 786432 | tf_op jit(solution)/shard_map/all_to_all | solution.py:418
  102.5 6.7 %first_half.1 = (f32[4,8,1024]{2,1,0:T(8,128)}, f32[4,8,1024]{2,1,0:T(8,128)}, f32[4,8,1024]{2,1,0:T(8,128)}, f32[4,8,1024]{2,1,0:T(8,128)}, f32[4,8,1024]{2,1,0...) custom-call(s32[4]{0:T(128)S(1)} %pad_add_fusion.at, ...), custom_call_target="tpu_custom_call" | custom-call | flops 8000000000 | tf_op jit(solution)/shard_map/first_half/pallas_call | solution.py:335
  109.8 2.7 %collective-permute-start.7 = (f32[4,8,1024]{2,1,0:T(8,128)}, f32[4,8,1024]{2,1,0:T(8,128)S(1)}, u32[]{:S(2)}, u32[]{:S(2)}) collective-permute-start(f32[4,8,1024]{2,1,0:T(8,128)} %get-tuple-element.111), channel_id=1, source_target_pairs={{0,56},{8,0},{16,8},{24,16},{32,24},{40,32},{48,40},{56,48},{1,57}... | collective-permute-start | bytes 393224 | tf_op jit(solution)/shard_map/ppermute | solution.py:414
  112.4 7.9 %second_half.1 = (f32[4,8,1024]{2,1,0:T(8,128)}, f32[4,8,1024]{2,1,0:T(8,128)}, f32[4,8,1024]{2,1,0:T(8,128)}, f32[4,8,1024]{2,1,0:T(8,128)}, f32[4,8,1024]{2,1,...) custom-call(s32[4]{0:T(128)S(1)} %pad_add_fusion.at, ...), custom_call_target="tpu_custom_call" | custom-call | flops 8000000000 | tf_op jit(solution)/shard_map/second_half/pallas_call | solution.py:335
  120.4 5.3 %all-to-all-start.7 = ((f32[32,32,512]{2,1,0:T(8,128)}), f32[32,32,512]{2,1,0:T(8,128)S(1)}, u32[]{:S(2)}, u32[]{:S(2)}) async-start(f32[32,32,512]{2,1,0:T(8,128)} %get-tuple-element.124), calls=%async_computation.7 | async-start | bytes 4194304 | tf_op jit(solution)/shard_map/all_to_all | solution.py:418
  125.9 2.1 %collective-permute-start.8 = (f32[4,8,1024]{2,1,0:T(8,128)S(1)}, f32[4,8,1024]{2,1,0:T(8,128)S(1)}, u32[]{:S(2)}, u32[]{:S(2)}) collective-permute-start(f32[4,8,1024]{2,1,0:T(8,128)S(1)} %add.32), channel_id=1, source_target_pairs={{0,8},{8,16},{16,24},{24,32},{32,40},{40,48},{48,56},{56,0},{1,9},... | collective-permute-start | bytes 393224 | tf_op jit(solution)/shard_map/ppermute | solution.py:414
  128.1 3.3 %collective-permute-done.16 = f32[4,8,1024]{2,1,0:T(8,128)S(1)} collective-permute-done((f32[4,8,1024]{2,1,0:T(8,128)S(1)}, f32[4,8,1024]{2,1,0:T(8,128)S(1)}, u32[]{:S(2)}, u32[]{:S(2)}) %collective-permute-start.16) | collective-permute-done | bytes 131104 | tf_op jit(solution)/shard_map/ppermute | solution.py:414
  131.5 1.6 collective-permute-start.17
  133.6 1.7 %collective-permute-start.9 = (f32[4,8,1024]{2,1,0:T(8,128)S(1)}, f32[4,8,1024]{2,1,0:T(8,128)S(1)}, u32[]{:S(2)}, u32[]{:S(2)}) collective-permute-start(f32[4,8,1024]{2,1,0:T(8,128)S(1)} %add.33), channel_id=1, source_target_pairs={{0,8},{8,16},{16,24},{24,32},{32,40},{40,48},{48,56},{56,0},{1,9},... | collective-permute-start | bytes 393224 | tf_op jit(solution)/shard_map/ppermute | solution.py:414
  136.2 1.7 %collective-permute-done.17 = f32[4,8,1024]{2,1,0:T(8,128)S(1)} collective-permute-done((f32[4,8,1024]{2,1,0:T(8,128)S(1)}, f32[4,8,1024]{2,1,0:T(8,128)S(1)}, u32[]{:S(2)}, u32[]{:S(2)}) %collective-permute-start.17) | collective-permute-done | bytes 131104 | tf_op jit(solution)/shard_map/ppermute | solution.py:414
  137.9 2.8 %collective-permute-start.18 = (f32[4,8,1024]{2,1,0:T(8,128)S(1)}, f32[4,8,1024]{2,1,0:T(8,128)S(1)}, u32[]{:S(2)}, u32[]{:S(2)}) collective-permute-start(f32[4,8,1024]{2,1,0:T(8,128)S(1)} %add.40), channel_id=1, source_target_pairs={{0,56},{8,0},{16,8},{24,16},{32,24},{40,32},{48,40},{56,48},{1,57}... | collective-permute-start | bytes 393224 | tf_op jit(solution)/shard_map/ppermute | solution.py:414
  140.8 1.5 collective-permute-start.12
  143.1 0.7 collective-permute-done.18
  143.9 3.8 %collective-permute-start.19 = (f32[4,8,1024]{2,1,0:T(8,128)S(1)}, f32[4,8,1024]{2,1,0:T(8,128)S(1)}, u32[]{:S(2)}, u32[]{:S(2)}) collective-permute-start(f32[4,8,1024]{2,1,0:T(8,128)S(1)} %add.41), channel_id=1, source_target_pairs={{0,56},{8,0},{16,8},{24,16},{32,24},{40,32},{48,40},{56,48},{1,57}... | collective-permute-start | bytes 393224 | tf_op jit(solution)/shard_map/ppermute | solution.py:414
  147.6 1.1 collective-permute-done.10.u0
  148.8 1.4 collective-permute-done.15.u1
  150.8 1.6 collective-permute-start.20
  152.4 2.8 %collective-permute-start.21 = (f32[8,2048]{1,0:T(8,128)S(1)}, f32[8,2048]{1,0:T(8,128)S(1)}, u32[]{:S(2)}, u32[]{:S(2)}) collective-permute-start(f32[8,2048]{1,0:T(8,128)S(1)} %get-tuple-element.144), channel_id=1, source_target_pairs={{0,128},{64,192},{128,0},{192,64},{1,129},{65,193},{129,1},{193,65... | collective-permute-start | bytes 196616 | tf_op jit(solution)/shard_map/ppermute | solution.py:414
  155.2 1.4 collective-permute-start.22
  156.6 1.6 collective-permute-done.21.refs_2_
  158.2 1.3 collective-permute-done.22.refs_3_
  159.4 1.3 proto_grad.1
  160.7 0.8 feat_grad.1
  (105 shorter events, 7.3 us)
Async XLA Ops:
  2.2 12.4 %all-to-all-start = ((f32[4,96,256]{2,1,0:T(8,128)}), f32[4,96,256]{2,1,0:T(8,128)S(1)}, u32[]{:S(2)}, u32[]{:S(2)}) async-start(f32[4,96,256]{2,1,0:T(8,128)} %broadcast_in_dim.2), calls=%async_computation | async-start | bytes 786432 | tf_op jit(solution)/shard_map/all_to_all | solution.py:418
  12.8 11.6 %copy-start.25 = (f32[248,256]{1,0:T(8,128)S(1)}, f32[248,256]{1,0:T(8,128)}, u32[]{:S(2)}) copy-start(f32[248,256]{1,0:T(8,128)} %get-tuple-element.84) | copy-start | bytes 761860
  15.9 16.8 %all-to-all-start.1 = ((f32[8,16,128]{2,1,0:T(8,128)}), f32[8,16,128]{2,1,0:T(8,128)S(1)}, u32[]{:S(2)}, u32[]{:S(2)}) async-start(f32[8,16,128]{2,1,0:T(8,128)} %get-tuple-element.80), calls=%async_computation.1 | async-start | bytes 131072 | tf_op jit(solution)/shard_map/all_to_all | solution.py:418
  24.3 23.2 %collective-permute-start.2 = (f32[248,256]{1,0:T(8,128)S(1)}, f32[248,256]{1,0:T(8,128)S(1)}, u32[]{:S(2)}, u32[]{:S(2)}) collective-permute-start(f32[248,256]{1,0:T(8,128)S(1)} %copy-done.25), channel_id=1, source_target_pairs={{0,128},{64,192},{128,0},{192,64},{1,129},{65,193},{129,1},{193,65... | collective-permute-start | bytes 761864 | tf_op jit(solution)/shard_map/ppermute | solution.py:414
  26.1 21.5 %collective-permute-start.1 = (f32[248,256]{1,0:T(8,128)S(1)}, f32[248,256]{1,0:T(8,128)S(1)}, u32[]{:S(2)}, u32[]{:S(2)}) collective-permute-start(f32[248,256]{1,0:T(8,128)S(1)} %copy-done.25), channel_id=1, source_target_pairs={{0,192},{64,0},{128,64},{192,128},{1,193},{65,1},{129,65},{193,129... | collective-permute-start | bytes 761864 | tf_op jit(solution)/shard_map/ppermute | solution.py:414
  27.7 19.9 %collective-permute-start = (f32[248,256]{1,0:T(8,128)S(1)}, f32[248,256]{1,0:T(8,128)S(1)}, u32[]{:S(2)}, u32[]{:S(2)}) collective-permute-start(f32[248,256]{1,0:T(8,128)S(1)} %copy-done.25), channel_id=1, source_target_pairs={{0,64},{64,128},{128,192},{192,0},{1,65},{65,129},{129,193},{193,1... | collective-permute-start | bytes 761864 | tf_op jit(solution)/shard_map/ppermute | solution.py:414
  34.1 12.8 %all-to-all-start.2 = ((f32[32,8,128]{2,1,0:T(8,128)}), f32[32,8,128]{2,1,0:T(8,128)S(1)}, u32[]{:S(2)}, u32[]{:S(2)}) async-start(f32[32,8,128]{2,1,0:T(8,128)} %row_sums.2), calls=%async_computation.2 | async-start | bytes 262144 | tf_op jit(solution)/shard_map/all_to_all | solution.py:418
  47.6 19.0 %copy-start.22 = (f32[248,256]{1,0:T(8,128)}, f32[248,256]{1,0:T(8,128)S(1)}, u32[]{:S(2)}) copy-start(f32[248,256]{1,0:T(8,128)S(1)} %collective-permute-done.2.mine_2) | copy-start | bytes 761860
  47.6 19.0 %copy-start.23 = (f32[248,256]{1,0:T(8,128)}, f32[248,256]{1,0:T(8,128)S(1)}, u32[]{:S(2)}) copy-start(f32[248,256]{1,0:T(8,128)S(1)} %collective-permute-done.1.mine_3) | copy-start | bytes 761860
  47.6 19.0 %copy-start.24 = (f32[248,256]{1,0:T(8,128)}, f32[248,256]{1,0:T(8,128)S(1)}, u32[]{:S(2)}) copy-start(f32[248,256]{1,0:T(8,128)S(1)} %collective-permute-done.mine_1) | copy-start | bytes 761860
  47.6 12.5 %collective-permute-start.3 = (f32[248,256]{1,0:T(8,128)S(1)}, f32[248,256]{1,0:T(8,128)S(1)}, u32[]{:S(2)}, u32[]{:S(2)}) collective-permute-start(f32[248,256]{1,0:T(8,128)S(1)} %collective-permute-done.mine_1), channel_id=1, source_target_pairs={{0,1},{1,0},{2,3},{3,2},{4,5},{5,4},{6,7},{7,6},{8,9},{9,8},{10,11... | collective-permute-start | bytes 761864 | tf_op jit(solution)/shard_map/ppermute | solution.py:414
  47.8 12.3 %collective-permute-start.5 = (f32[248,256]{1,0:T(8,128)S(1)}, f32[248,256]{1,0:T(8,128)S(1)}, u32[]{:S(2)}, u32[]{:S(2)}) collective-permute-start(f32[248,256]{1,0:T(8,128)S(1)} %collective-permute-done.2.mine_2), channel_id=1, source_target_pairs={{0,1},{1,0},{2,3},{3,2},{4,5},{5,4},{6,7},{7,6},{8,9},{9,8},{10,11... | collective-permute-start | bytes 761864 | tf_op jit(solution)/shard_map/ppermute | solution.py:414
  48.2 11.9 %collective-permute-start.4 = (f32[248,256]{1,0:T(8,128)S(1)}, f32[248,256]{1,0:T(8,128)S(1)}, u32[]{:S(2)}, u32[]{:S(2)}) collective-permute-start(f32[248,256]{1,0:T(8,128)S(1)} %collective-permute-done.1.mine_3), channel_id=1, source_target_pairs={{0,1},{1,0},{2,3},{3,2},{4,5},{5,4},{6,7},{7,6},{8,9},{9,8},{10,11... | collective-permute-start | bytes 761864 | tf_op jit(solution)/shard_map/ppermute | solution.py:414
  61.6 11.7 %all-to-all-start.4 = ((f32[32,8,128]{2,1,0:T(8,128)}), f32[32,8,128]{2,1,0:T(8,128)S(1)}, u32[]{:S(2)}, u32[]{:S(2)}) async-start(f32[32,8,128]{2,1,0:T(8,128)} %row_sums.3), calls=%async_computation.4 | async-start | bytes 262144 | tf_op jit(solution)/shard_map/all_to_all | solution.py:418
  74.6 11.7 %all-to-all-start.5 = ((f32[8,16,128]{2,1,0:T(8,128)}), f32[8,16,128]{2,1,0:T(8,128)S(1)}, u32[]{:S(2)}, u32[]{:S(2)}) async-start(f32[8,16,128]{2,1,0:T(8,128)} %col_sums.3), calls=%async_computation.5 | async-start | bytes 131072 | tf_op jit(solution)/shard_map/all_to_all | solution.py:418
  82.3 20.2 %copy-start.11 = (f32[4,8,512]{2,1,0:T(8,128)S(1)}, f32[4,8,512]{2,1,0:T(8,128)}, u32[]{:S(2)}) copy-start(f32[4,8,512]{2,1,0:T(8,128)} %get-tuple-element.94.crops) | copy-start | bytes 196612
  86.2 16.2 %copy-start.2 = (bf16[256,2048]{1,0:T(8,128)(2,1)S(1)}, bf16[256,2048]{1,0:T(8,128)(2,1)}, u32[]{:S(2)}) copy-start(bf16[256,2048]{1,0:T(8,128)(2,1)} %get-tuple-element.109.tn) | copy-start | bytes 3145732
  86.2 16.2 %copy-start.7 = (bf16[4,256,480]{2,1,0:T(8,128)(2,1)S(1)}, bf16[4,256,480]{2,1,0:T(8,128)(2,1)}, u32[]{:S(2)}) copy-start(bf16[4,256,480]{2,1,0:T(8,128)(2,1)} %get-tuple-element.106.ubt) | copy-start | bytes 2949124
  86.2 16.3 %copy-start.9 = (bf16[1920,256]{1,0:T(8,128)(2,1)S(1)}, bf16[1920,256]{1,0:T(8,128)(2,1)}, u32[]{:S(2)}) copy-start(bf16[1920,256]{1,0:T(8,128)(2,1)} %get-tuple-element.103.ub) | copy-start | bytes 2949124
  86.2 16.3 %copy-start.10 = (bf16[1920,256]{1,0:T(8,128)(2,1)S(1)}, bf16[1920,256]{1,0:T(8,128)(2,1)}, u32[]{:S(2)}) copy-start(bf16[1920,256]{1,0:T(8,128)(2,1)} %get-tuple-element.107.tuc) | copy-start | bytes 2949124
  109.2 11.1 %collective-permute-start.6 = (f32[4,8,1024]{2,1,0:T(8,128)}, f32[4,8,1024]{2,1,0:T(8,128)S(1)}, u32[]{:S(2)}, u32[]{:S(2)}) collective-permute-start(f32[4,8,1024]{2,1,0:T(8,128)} %get-tuple-element.110), channel_id=1, source_target_pairs={{0,8},{8,16},{16,24},{24,32},{32,40},{40,48},{48,56},{56,0},{1,9},... | collective-permute-start | bytes 393224 | tf_op jit(solution)/shard_map/ppermute | solution.py:414
  109.8 10.5 %collective-permute-start.7 = (f32[4,8,1024]{2,1,0:T(8,128)}, f32[4,8,1024]{2,1,0:T(8,128)S(1)}, u32[]{:S(2)}, u32[]{:S(2)}) collective-permute-start(f32[4,8,1024]{2,1,0:T(8,128)} %get-tuple-element.111), channel_id=1, source_target_pairs={{0,56},{8,0},{16,8},{24,16},{32,24},{40,32},{48,40},{56,48},{1,57}... | collective-permute-start | bytes 393224 | tf_op jit(solution)/shard_map/ppermute | solution.py:414
  120.4 12.7 %copy-start.19 = (f32[4,8,1024]{2,1,0:T(8,128)S(1)}, f32[4,8,1024]{2,1,0:T(8,128)}, u32[]{:S(2)}) copy-start(f32[4,8,1024]{2,1,0:T(8,128)} %get-tuple-element.132) | copy-start | bytes 393220
  120.4 13.2 %copy-start.17 = (f32[4,8,1024]{2,1,0:T(8,128)S(1)}, f32[4,8,1024]{2,1,0:T(8,128)}, u32[]{:S(2)}) copy-start(f32[4,8,1024]{2,1,0:T(8,128)} %get-tuple-element.129) | copy-start | bytes 393220
  120.4 15.2 %copy-start.18 = (f32[4,8,1024]{2,1,0:T(8,128)S(1)}, f32[4,8,1024]{2,1,0:T(8,128)}, u32[]{:S(2)}) copy-start(f32[4,8,1024]{2,1,0:T(8,128)} %get-tuple-element.136) | copy-start | bytes 393220
  120.4 17.5 %copy-start.16 = (f32[4,8,1024]{2,1,0:T(8,128)S(1)}, f32[4,8,1024]{2,1,0:T(8,128)}, u32[]{:S(2)}) copy-start(f32[4,8,1024]{2,1,0:T(8,128)} %get-tuple-element.140) | copy-start | bytes 393220
  120.4 40.3 %all-to-all-start.7 = ((f32[32,32,512]{2,1,0:T(8,128)}), f32[32,32,512]{2,1,0:T(8,128)S(1)}, u32[]{:S(2)}, u32[]{:S(2)}) async-start(f32[32,32,512]{2,1,0:T(8,128)} %get-tuple-element.124), calls=%async_computation.7 | async-start | bytes 4194304 | tf_op jit(solution)/shard_map/all_to_all | solution.py:418
  125.7 15.0 %copy-start.15 = (f32[4,8,1024]{2,1,0:T(8,128)S(1)}, f32[4,8,1024]{2,1,0:T(8,128)}, u32[]{:S(2)}) copy-start(f32[4,8,1024]{2,1,0:T(8,128)} %get-tuple-element.133) | copy-start | bytes 393220
  125.8 16.5 %copy-start.13 = (f32[4,8,1024]{2,1,0:T(8,128)S(1)}, f32[4,8,1024]{2,1,0:T(8,128)}, u32[]{:S(2)}) copy-start(f32[4,8,1024]{2,1,0:T(8,128)} %get-tuple-element.130) | copy-start | bytes 393220
  125.8 17.2 %copy-start.14 = (f32[4,8,1024]{2,1,0:T(8,128)S(1)}, f32[4,8,1024]{2,1,0:T(8,128)}, u32[]{:S(2)}) copy-start(f32[4,8,1024]{2,1,0:T(8,128)} %get-tuple-element.137) | copy-start | bytes 393220
  125.8 18.1 %copy-start.12 = (f32[4,8,1024]{2,1,0:T(8,128)S(1)}, f32[4,8,1024]{2,1,0:T(8,128)}, u32[]{:S(2)}) copy-start(f32[4,8,1024]{2,1,0:T(8,128)} %get-tuple-element.141) | copy-start | bytes 393220
  125.8 24.4 %copy-start.5 = (f32[4,8,1024]{2,1,0:T(8,128)S(1)}, f32[4,8,1024]{2,1,0:T(8,128)}, u32[]{:S(2)}) copy-start(f32[4,8,1024]{2,1,0:T(8,128)} %get-tuple-element.126.p0) | copy-start | bytes 393220
  125.8 24.4 %copy-start.6 = (f32[4,8,1024]{2,1,0:T(8,128)S(1)}, f32[4,8,1024]{2,1,0:T(8,128)}, u32[]{:S(2)}) copy-start(f32[4,8,1024]{2,1,0:T(8,128)} %get-tuple-element.134.p1) | copy-start | bytes 393220
  125.8 5.6 %collective-permute-start.16 = (f32[4,8,1024]{2,1,0:T(8,128)S(1)}, f32[4,8,1024]{2,1,0:T(8,128)S(1)}, u32[]{:S(2)}, u32[]{:S(2)}) collective-permute-start(f32[4,8,1024]{2,1,0:T(8,128)S(1)} %copy-done.30), channel_id=1, source_target_pairs={{0,56},{8,0},{16,8},{24,16},{32,24},{40,32},{48,40},{56,48},{1,57}... | collective-permute-start | bytes 393224 | tf_op jit(solution)/shard_map/ppermute | solution.py:414
  125.9 7.6 %collective-permute-start.8 = (f32[4,8,1024]{2,1,0:T(8,128)S(1)}, f32[4,8,1024]{2,1,0:T(8,128)S(1)}, u32[]{:S(2)}, u32[]{:S(2)}) collective-permute-start(f32[4,8,1024]{2,1,0:T(8,128)S(1)} %add.32), channel_id=1, source_target_pairs={{0,8},{8,16},{16,24},{24,32},{32,40},{40,48},{48,56},{56,0},{1,9},... | collective-permute-start | bytes 393224 | tf_op jit(solution)/shard_map/ppermute | solution.py:414
  128.0 7.6 %collective-permute-start.13 = (f32[4,8,1024]{2,1,0:T(8,128)S(1)}, f32[4,8,1024]{2,1,0:T(8,128)S(1)}, u32[]{:S(2)}, u32[]{:S(2)}) collective-permute-start(f32[4,8,1024]{2,1,0:T(8,128)S(1)} %copy-done.29), channel_id=1, source_target_pairs={{0,8},{8,16},{16,24},{24,32},{32,40},{40,48},{48,56},{56,0},{1,9},... | collective-permute-start | bytes 393224 | tf_op jit(solution)/shard_map/ppermute | solution.py:414
  131.5 6.4 %collective-permute-start.17 = (f32[4,8,1024]{2,1,0:T(8,128)S(1)}, f32[4,8,1024]{2,1,0:T(8,128)S(1)}, u32[]{:S(2)}, u32[]{:S(2)}) collective-permute-start(f32[4,8,1024]{2,1,0:T(8,128)S(1)} %add.39), channel_id=1, source_target_pairs={{0,56},{8,0},{16,8},{24,16},{32,24},{40,32},{48,40},{56,48},{1,57}... | collective-permute-start | bytes 393224 | tf_op jit(solution)/shard_map/ppermute | solution.py:414
  133.1 7.7 %collective-permute-start.11 = (f32[4,8,1024]{2,1,0:T(8,128)S(1)}, f32[4,8,1024]{2,1,0:T(8,128)S(1)}, u32[]{:S(2)}, u32[]{:S(2)}) collective-permute-start(f32[4,8,1024]{2,1,0:T(8,128)S(1)} %add.35), channel_id=1, source_target_pairs={{0,56},{8,0},{16,8},{24,16},{32,24},{40,32},{48,40},{56,48},{1,57}... | collective-permute-start | bytes 393224 | tf_op jit(solution)/shard_map/ppermute | solution.py:414
  133.6 8.7 %collective-permute-start.9 = (f32[4,8,1024]{2,1,0:T(8,128)S(1)}, f32[4,8,1024]{2,1,0:T(8,128)S(1)}, u32[]{:S(2)}, u32[]{:S(2)}) collective-permute-start(f32[4,8,1024]{2,1,0:T(8,128)S(1)} %add.33), channel_id=1, source_target_pairs={{0,8},{8,16},{16,24},{24,32},{32,40},{40,48},{48,56},{56,0},{1,9},... | collective-permute-start | bytes 393224 | tf_op jit(solution)/shard_map/ppermute | solution.py:414
  135.6 7.4 %collective-permute-start.14 = (f32[4,8,1024]{2,1,0:T(8,128)S(1)}, f32[4,8,1024]{2,1,0:T(8,128)S(1)}, u32[]{:S(2)}, u32[]{:S(2)}) collective-permute-start(f32[4,8,1024]{2,1,0:T(8,128)S(1)} %add.37), channel_id=1, source_target_pairs={{0,8},{8,16},{16,24},{24,32},{32,40},{40,48},{48,56},{56,0},{1,9},... | collective-permute-start | bytes 393224 | tf_op jit(solution)/shard_map/ppermute | solution.py:414
  137.9 5.9 %collective-permute-start.18 = (f32[4,8,1024]{2,1,0:T(8,128)S(1)}, f32[4,8,1024]{2,1,0:T(8,128)S(1)}, u32[]{:S(2)}, u32[]{:S(2)}) collective-permute-start(f32[4,8,1024]{2,1,0:T(8,128)S(1)} %add.40), channel_id=1, source_target_pairs={{0,56},{8,0},{16,8},{24,16},{32,24},{40,32},{48,40},{56,48},{1,57}... | collective-permute-start | bytes 393224 | tf_op jit(solution)/shard_map/ppermute | solution.py:414
  140.8 6.9 %collective-permute-start.12 = (f32[4,8,1024]{2,1,0:T(8,128)S(1)}, f32[4,8,1024]{2,1,0:T(8,128)S(1)}, u32[]{:S(2)}, u32[]{:S(2)}) collective-permute-start(f32[4,8,1024]{2,1,0:T(8,128)S(1)} %add.36), channel_id=1, source_target_pairs={{0,56},{8,0},{16,8},{24,16},{32,24},{40,32},{48,40},{56,48},{1,57}... | collective-permute-start | bytes 393224 | tf_op jit(solution)/shard_map/ppermute | solution.py:414
  142.3 6.5 %collective-permute-start.10 = (f32[4,8,1024]{2,1,0:T(8,128)S(1)}, f32[4,8,1024]{2,1,0:T(8,128)S(1)}, u32[]{:S(2)}, u32[]{:S(2)}) collective-permute-start(f32[4,8,1024]{2,1,0:T(8,128)S(1)} %add.34), channel_id=1, source_target_pairs={{0,8},{8,16},{16,24},{24,32},{32,40},{40,48},{48,56},{56,0},{1,9},... | collective-permute-start | bytes 393224 | tf_op jit(solution)/shard_map/ppermute | solution.py:414
  143.0 7.2 %collective-permute-start.15 = (f32[4,8,1024]{2,1,0:T(8,128)S(1)}, f32[4,8,1024]{2,1,0:T(8,128)S(1)}, u32[]{:S(2)}, u32[]{:S(2)}) collective-permute-start(f32[4,8,1024]{2,1,0:T(8,128)S(1)} %add.38), channel_id=1, source_target_pairs={{0,8},{8,16},{16,24},{24,32},{32,40},{40,48},{48,56},{56,0},{1,9},... | collective-permute-start | bytes 393224 | tf_op jit(solution)/shard_map/ppermute | solution.py:414
  143.9 6.3 %collective-permute-start.19 = (f32[4,8,1024]{2,1,0:T(8,128)S(1)}, f32[4,8,1024]{2,1,0:T(8,128)S(1)}, u32[]{:S(2)}, u32[]{:S(2)}) collective-permute-start(f32[4,8,1024]{2,1,0:T(8,128)S(1)} %add.41), channel_id=1, source_target_pairs={{0,56},{8,0},{16,8},{24,16},{32,24},{40,32},{48,40},{56,48},{1,57}... | collective-permute-start | bytes 393224 | tf_op jit(solution)/shard_map/ppermute | solution.py:414
  150.8 5.8 %collective-permute-start.20 = (f32[8,2048]{1,0:T(8,128)S(1)}, f32[8,2048]{1,0:T(8,128)S(1)}, u32[]{:S(2)}, u32[]{:S(2)}) collective-permute-start(f32[8,2048]{1,0:T(8,128)S(1)} %get-tuple-element.143), channel_id=1, source_target_pairs={{0,64},{64,128},{128,192},{192,0},{1,65},{65,129},{129,193},{193,1... | collective-permute-start | bytes 196616 | tf_op jit(solution)/shard_map/ppermute | solution.py:414
  152.4 5.8 %collective-permute-start.21 = (f32[8,2048]{1,0:T(8,128)S(1)}, f32[8,2048]{1,0:T(8,128)S(1)}, u32[]{:S(2)}, u32[]{:S(2)}) collective-permute-start(f32[8,2048]{1,0:T(8,128)S(1)} %get-tuple-element.144), channel_id=1, source_target_pairs={{0,128},{64,192},{128,0},{192,64},{1,129},{65,193},{129,1},{193,65... | collective-permute-start | bytes 196616 | tf_op jit(solution)/shard_map/ppermute | solution.py:414
  155.2 4.3 %collective-permute-start.22 = (f32[8,2048]{1,0:T(8,128)S(1)}, f32[8,2048]{1,0:T(8,128)S(1)}, u32[]{:S(2)}, u32[]{:S(2)}) collective-permute-start(f32[8,2048]{1,0:T(8,128)S(1)} %get-tuple-element.145), channel_id=1, source_target_pairs={{0,192},{64,0},{128,64},{192,128},{1,193},{65,1},{129,65},{193,129... | collective-permute-start | bytes 196616 | tf_op jit(solution)/shard_map/ppermute | solution.py:414
  (12 other events, 76.5 us)
where the time goes:
time: 162 us; the launch traced here: 161 us
  starting transfers between devices  61.3 us (38%)
  Pallas kernels  40.1 us (25%)
  blocking collectives  27.3 us (17%)
  waiting for transfers between devices  26.8 us (17%)
  local copies, waits for them, and re-layouts  3.94 us (2%)
    all_to_all x6, starting transfers between devices, exchange(): return lax.all_to_all(v, axes, 0, 0, tiled=False)  32.6 us
    ppermute x23, starting transfers between devices, shift(): return lax.ppermute(v, axis, [(i, (i + d) % size) for i in range(size)])  28.6 us
    all_to_all x2, blocking collectives, exchange(): return lax.all_to_all(v, axes, 0, 0, tiled=False)  27.3 us
    all_to_all x6, waiting for transfers between devices, exchange(): return lax.all_to_all(v, axes, 0, 0, tiled=False)  14.9 us
    pallas_call x2, Pallas kernels, grad_call(): pl.pallas_call(kernel, grid_spec=pltpu.PrefetchScalarGridSpec(num_scalar_...  14.5 us
    ppermute x23, waiting for transfers between devices, shift(): return lax.ppermute(v, axis, [(i, (i + d) % size) for i in range(size)])  11.9 us
    pallas_call x1, Pallas kernels, rows_pass(): pl.pallas_call(rows_kernel, grid_spec=pltpu.PrefetchScalarGridSpec(num_sc...  5.87 us
    pallas_call x2, Pallas kernels, norm_pass(): pl.pallas_call(norm_kernel, grid_spec=pltpu.PrefetchScalarGridSpec(num_sc...  5.82 us
  transfers between devices with their start and end apart: 29, of which 14 were waited for; matrix products, arithmetic and copies ran while one was open for 1% of the time, Pallas kernels for 17%

commit v1 on v0

--- a/solution.py
+++ b/solution.py
@@ -472,8 +472,10 @@
     u0, d1 = up(u0 + p0[1]), down(d1 + p1[7])
     own, *give = merge_pass(at, p0[0], u0, d0, p1[0], u1, d1)
     got = [shift(v, "x", NX, d) for v, d in zip(give, (1, 2, 3))]
+    feat_grad = feat_pass(g, mine)
+    feat_grad, *got = together((feat_grad, *got))
     proto_grad = proto_pass(at, own, *got)
-    feat_grad = feat_pass(g, mine).T
+    feat_grad = feat_grad.T
     return (feat_grad, proto_grad)
 
 

time: 162 us -> 162 us (level)
  no operation moved by 1% of the time
where the time goes in v1:
time: 162 us; the launch traced here: 161 us
  starting transfers between devices  61.3 us (38%)
  Pallas kernels  40.1 us (25%)
  blocking collectives  27.3 us (17%)
  waiting for transfers between devices  26 us (16%)
  local copies, waits for them, and re-layouts  3.94 us (2%)
    all_to_all x6, starting transfers between devices, exchange(): return lax.all_to_all(v, axes, 0, 0, tiled=False)  32.6 us
    ppermute x23, starting transfers between devices, shift(): return lax.ppermute(v, axis, [(i, (i + d) % size) for i in range(size)])  28.6 us
    all_to_all x2, blocking collectives, exchange(): return lax.all_to_all(v, axes, 0, 0, tiled=False)  27.3 us
    all_to_all x6, waiting for transfers between devices, exchange(): return lax.all_to_all(v, axes, 0, 0, tiled=False)  14.9 us
    pallas_call x2, Pallas kernels, grad_call(): pl.pallas_call(kernel, grid_spec=pltpu.PrefetchScalarGridSpec(num_scalar_...  14.5 us
    ppermute x23, waiting for transfers between devices, shift(): return lax.ppermute(v, axis, [(i, (i + d) % size) for i in range(size)])  11.1 us
    pallas_call x1, Pallas kernels, rows_pass(): pl.pallas_call(rows_kernel, grid_spec=pltpu.PrefetchScalarGridSpec(num_sc...  5.87 us
    pallas_call x2, Pallas kernels, norm_pass(): pl.pallas_call(norm_kernel, grid_spec=pltpu.PrefetchScalarGridSpec(num_sc...  5.82 us
  transfers between devices with their start and end apart: 29, of which 14 were waited for; matrix products, arithmetic and copies ran while one was open for 1% of the time, Pallas kernels for 17%

profile of v1, /device:TPU:8, one launch (start us, length us, event | category | flops | bytes accessed | tf_op | source)
XLA Modules:
  0.0 160.7 jit_solution(127630128599810917)
XLA Ops:
  0.6 1.6 broadcast_in_dim.2
  2.2 4.3 %all-to-all-start = ((f32[4,96,256]{2,1,0:T(8,128)}), f32[4,96,256]{2,1,0:T(8,128)S(1)}, u32[]{:S(2)}, u32[]{:S(2)}) async-start(f32[4,96,256]{2,1,0:T(8,128)} %broadcast_in_dim.2), calls=%async_computation | async-start | bytes 786432 | tf_op jit(solution)/shard_map/all_to_all | solution.py:418
  7.4 0.9 copy-done
  8.3 1.4 pack_rows.1
  9.7 3.0 %teacher_norm.1 = (bf16[256,2048]{1,0:T(8,128)(2,1)}, bf16[256,2048]{1,0:T(8,128)(2,1)S(1)}) custom-call(s32[4]{0:T(128)S(1)} %pad_add_fusion.at, bf16[256,8192]{1,0:T(8,128)(2,1)} %w.2), custom_call_target="tpu_custom_call" | custom-call | flops 2000000000 | tf_op jit(solution)/shard_map/teacher_norm/pallas_call | solution.py:88
  12.8 1.8 %all-to-all-done.tf = f32[4,96,256]{2,1,0:T(8,128)S(1)} async-done(((f32[4,96,256]{2,1,0:T(8,128)}), f32[4,96,256]{2,1,0:T(8,128)S(1)}, u32[]{:S(2)}, u32[]{:S(2)}) %all-to-all-start) | async-done | bytes 393248 | tf_op jit(solution)/shard_map/all_to_all | solution.py:418
  14.6 1.3 teacher_scores.1
  15.9 8.5 %all-to-all-start.1 = ((f32[8,16,128]{2,1,0:T(8,128)}), f32[8,16,128]{2,1,0:T(8,128)S(1)}, u32[]{:S(2)}, u32[]{:S(2)}) async-start(f32[8,16,128]{2,1,0:T(8,128)} %get-tuple-element.84), calls=%async_computation.1 | async-start | bytes 131072 | tf_op jit(solution)/shard_map/all_to_all | solution.py:418
  24.3 1.8 %collective-permute-start.2 = (f32[248,256]{1,0:T(8,128)S(1)}, f32[248,256]{1,0:T(8,128)S(1)}, u32[]{:S(2)}, u32[]{:S(2)}) collective-permute-start(f32[248,256]{1,0:T(8,128)S(1)} %copy-done.25), channel_id=1, source_target_pairs={{0,128},{64,192},{128,0},{192,64},{1,129},{65,193},{129,1},{193,65... | collective-permute-start | bytes 761864 | tf_op jit(solution)/shard_map/ppermute | solution.py:414
  26.1 1.5 collective-permute-start.1
  28.2 4.6 %all-to-all-done.1.c_parts = f32[8,16,128]{2,1,0:T(8,128)S(1)} async-done(((f32[8,16,128]{2,1,0:T(8,128)}), f32[8,16,128]{2,1,0:T(8,128)S(1)}, u32[]{:S(2)}, u32[]{:S(2)}) %all-to-all-start.1) | async-done | bytes 65568 | tf_op jit(solution)/shard_map/all_to_all | solution.py:418
  32.7 1.4 row_sums.2
  34.1 6.2 %all-to-all-start.2 = ((f32[32,8,128]{2,1,0:T(8,128)}), f32[32,8,128]{2,1,0:T(8,128)S(1)}, u32[]{:S(2)}, u32[]{:S(2)}) async-start(f32[32,8,128]{2,1,0:T(8,128)} %row_sums.2), calls=%async_computation.2 | async-start | bytes 262144 | tf_op jit(solution)/shard_map/all_to_all | solution.py:418
  40.3 2.8 %student_norm.1.sn = bf16[256,2048]{1,0:T(8,128)(2,1)} custom-call(s32[4]{0:T(128)S(1)} %pad_add_fusion.at, bf16[256,8192]{1,0:T(8,128)(2,1)} %w.3), custom_call_target="tpu_custom_call" | custom-call | flops 2000000000 | tf_op jit(solution)/shard_map/student_norm/pallas_call | solution.py:88
  43.1 3.8 %all-to-all-done.2.r_parts = f32[32,8,128]{2,1,0:T(8,128)S(1)} async-done(((f32[32,8,128]{2,1,0:T(8,128)}), f32[32,8,128]{2,1,0:T(8,128)S(1)}, u32[]{:S(2)}, u32[]{:S(2)}) %all-to-all-start.2) | async-done | bytes 131104 | tf_op jit(solution)/shard_map/all_to_all | solution.py:418
  48.4 11.8 %all_to_all.40.c_parts = f32[8,16,128]{2,1,0:T(8,128)S(1)} all-to-all(f32[8,16,128]{2,1,0:T(8,128)S(1)} %col_sums.2), channel_id=1, replica_groups=mesh['x'=4,'z'=8,'y'=4,'c'=2] {'z'}, dimensions={0} | all-to-all | bytes 131072 | tf_op jit(solution)/shard_map/all_to_all | solution.py:418
  60.2 1.4 row_sums.3
  61.6 5.0 %all-to-all-start.4 = ((f32[32,8,128]{2,1,0:T(8,128)}), f32[32,8,128]{2,1,0:T(8,128)S(1)}, u32[]{:S(2)}, u32[]{:S(2)}) async-start(f32[32,8,128]{2,1,0:T(8,128)} %row_sums.3), calls=%async_computation.4 | async-start | bytes 262144 | tf_op jit(solution)/shard_map/all_to_all | solution.py:418
  66.6 5.9 %student_units.1 = (bf16[1920,256]{1,0:T(8,128)(2,1)}, bf16[4,256,480]{2,1,0:T(8,128)(2,1)}, f32[4,256,480]{2,1,0:T(8,128)}, bf16[1920,256]{1,0:T(8,128)(2,1)}, f32[4,8,512]{2,1,0:T(8,128)}, /*index=5*/f32[40,480]{1,0:T(8,128)}) custom-call(s32[4]{0:T(128)S(1)} %pad_add_fusion.at, f32[488,256]{1,0:T(8,128)} %get-tuple-element.81.own, f32[248,256]{1,0:T(8,128)} %copy-done.24, ...), custom_call_target="tpu_custom_call" | custom-call | flops 3000000000 | tf_op jit(solution)/shard_map/student_units/pallas_call | solution.py:225
  72.5 0.8 all-to-all-done.4.r_parts
  73.3 1.3 col_sums.3
  74.6 3.4 %all-to-all-start.5 = ((f32[8,16,128]{2,1,0:T(8,128)}), f32[8,16,128]{2,1,0:T(8,128)S(1)}, u32[]{:S(2)}, u32[]{:S(2)}) async-start(f32[8,16,128]{2,1,0:T(8,128)} %col_sums.3), calls=%async_computation.5 | async-start | bytes 131072 | tf_op jit(solution)/shard_map/all_to_all | solution.py:418
  78.0 1.2 copy-done.8
  79.1 3.1 %student_sums.1.refs_0_ = f32[16,128]{1,0:T(8,128)S(1)} custom-call(bf16[1920,256]{1,0:T(8,128)(2,1)S(1)} %copy-done.8, bf16[256,2048]{1,0:T(8,128)(2,1)S(1)} %copy-done.1), custom_call_target="tpu_custom_call" | custom-call | flops 3000000000 | tf_op jit(solution)/shard_map/student_sums/pallas_call | solution.py:260
  82.3 4.0 %all-to-all-done.5.c_parts = f32[8,16,128]{2,1,0:T(8,128)S(1)} async-done(((f32[8,16,128]{2,1,0:T(8,128)}), f32[8,16,128]{2,1,0:T(8,128)S(1)}, u32[]{:S(2)}, u32[]{:S(2)}) %all-to-all-start.5) | async-done | bytes 65568 | tf_op jit(solution)/shard_map/all_to_all | solution.py:418
  87.0 15.5 %all_to_all.41.parts = f32[32,24,128]{2,1,0:T(8,128)S(1)} all-to-all(f32[32,24,128]{2,1,0:T(8,128)S(1)} %get-tuple-element.109), channel_id=1, replica_groups=mesh['x'=4,'z'=8,'y'=4,'c'=2] {'x','y','c'}, dimensions={0} | all-to-all | bytes 786432 | tf_op jit(solution)/shard_map/all_to_all | solution.py:418
  102.5 6.7 %first_half.1 = (f32[4,8,1024]{2,1,0:T(8,128)}, f32[4,8,1024]{2,1,0:T(8,128)}, f32[4,8,1024]{2,1,0:T(8,128)}, f32[4,8,1024]{2,1,0:T(8,128)}, f32[4,8,1024]{2,1,0...) custom-call(s32[4]{0:T(128)S(1)} %pad_add_fusion.at, ...), custom_call_target="tpu_custom_call" | custom-call | flops 8000000000 | tf_op jit(solution)/shard_map/first_half/pallas_call | solution.py:335
  109.8 2.7 %collective-permute-start.7 = (f32[4,8,1024]{2,1,0:T(8,128)}, f32[4,8,1024]{2,1,0:T(8,128)S(1)}, u32[]{:S(2)}, u32[]{:S(2)}) collective-permute-start(f32[4,8,1024]{2,1,0:T(8,128)} %get-tuple-element.115), channel_id=1, source_target_pairs={{0,56},{8,0},{16,8},{24,16},{32,24},{40,32},{48,40},{56,48},{1,57}... | collective-permute-start | bytes 393224 | tf_op jit(solution)/shard_map/ppermute | solution.py:414
  112.4 7.9 %second_half.1 = (f32[4,8,1024]{2,1,0:T(8,128)}, f32[4,8,1024]{2,1,0:T(8,128)}, f32[4,8,1024]{2,1,0:T(8,128)}, f32[4,8,1024]{2,1,0:T(8,128)}, f32[4,8,1024]{2,1,...) custom-call(s32[4]{0:T(128)S(1)} %pad_add_fusion.at, ...), custom_call_target="tpu_custom_call" | custom-call | flops 8000000000 | tf_op jit(solution)/shard_map/second_half/pallas_call | solution.py:335
  120.4 5.3 %all-to-all-start.7 = ((f32[32,32,512]{2,1,0:T(8,128)}), f32[32,32,512]{2,1,0:T(8,128)S(1)}, u32[]{:S(2)}, u32[]{:S(2)}) async-start(f32[32,32,512]{2,1,0:T(8,128)} %get-tuple-element.128), calls=%async_computation.7 | async-start | bytes 4194304 | tf_op jit(solution)/shard_map/all_to_all | solution.py:418
  125.9 2.1 %collective-permute-start.8 = (f32[4,8,1024]{2,1,0:T(8,128)S(1)}, f32[4,8,1024]{2,1,0:T(8,128)S(1)}, u32[]{:S(2)}, u32[]{:S(2)}) collective-permute-start(f32[4,8,1024]{2,1,0:T(8,128)S(1)} %add.32), channel_id=1, source_target_pairs={{0,8},{8,16},{16,24},{24,32},{32,40},{40,48},{48,56},{56,0},{1,9},... | collective-permute-start | bytes 393224 | tf_op jit(solution)/shard_map/ppermute | solution.py:414
  128.1 3.3 %collective-permute-done.16 = f32[4,8,1024]{2,1,0:T(8,128)S(1)} collective-permute-done((f32[4,8,1024]{2,1,0:T(8,128)S(1)}, f32[4,8,1024]{2,1,0:T(8,128)S(1)}, u32[]{:S(2)}, u32[]{:S(2)}) %collective-permute-start.16) | collective-permute-done | bytes 131104 | tf_op jit(solution)/shard_map/ppermute | solution.py:414
  131.5 1.6 collective-permute-start.17
  133.6 1.7 %collective-permute-start.9 = (f32[4,8,1024]{2,1,0:T(8,128)S(1)}, f32[4,8,1024]{2,1,0:T(8,128)S(1)}, u32[]{:S(2)}, u32[]{:S(2)}) collective-permute-start(f32[4,8,1024]{2,1,0:T(8,128)S(1)} %add.33), channel_id=1, source_target_pairs={{0,8},{8,16},{16,24},{24,32},{32,40},{40,48},{48,56},{56,0},{1,9},... | collective-permute-start | bytes 393224 | tf_op jit(solution)/shard_map/ppermute | solution.py:414
  136.2 1.7 %collective-permute-done.17 = f32[4,8,1024]{2,1,0:T(8,128)S(1)} collective-permute-done((f32[4,8,1024]{2,1,0:T(8,128)S(1)}, f32[4,8,1024]{2,1,0:T(8,128)S(1)}, u32[]{:S(2)}, u32[]{:S(2)}) %collective-permute-start.17) | collective-permute-done | bytes 131104 | tf_op jit(solution)/shard_map/ppermute | solution.py:414
  137.9 2.8 %collective-permute-start.18 = (f32[4,8,1024]{2,1,0:T(8,128)S(1)}, f32[4,8,1024]{2,1,0:T(8,128)S(1)}, u32[]{:S(2)}, u32[]{:S(2)}) collective-permute-start(f32[4,8,1024]{2,1,0:T(8,128)S(1)} %add.40), channel_id=1, source_target_pairs={{0,56},{8,0},{16,8},{24,16},{32,24},{40,32},{48,40},{56,48},{1,57}... | collective-permute-start | bytes 393224 | tf_op jit(solution)/shard_map/ppermute | solution.py:414
  140.8 1.5 collective-permute-start.12
  143.1 0.7 collective-permute-done.18
  143.9 3.8 %collective-permute-start.19 = (f32[4,8,1024]{2,1,0:T(8,128)S(1)}, f32[4,8,1024]{2,1,0:T(8,128)S(1)}, u32[]{:S(2)}, u32[]{:S(2)}) collective-permute-start(f32[4,8,1024]{2,1,0:T(8,128)S(1)} %add.41), channel_id=1, source_target_pairs={{0,56},{8,0},{16,8},{24,16},{32,24},{40,32},{48,40},{56,48},{1,57}... | collective-permute-start | bytes 393224 | tf_op jit(solution)/shard_map/ppermute | solution.py:414
  147.6 1.1 collective-permute-done.10.u0
  148.8 1.4 collective-permute-done.15.u1
  150.8 1.6 collective-permute-start.20
  152.4 2.8 %collective-permute-start.21 = (f32[8,2048]{1,0:T(8,128)S(1)}, f32[8,2048]{1,0:T(8,128)S(1)}, u32[]{:S(2)}, u32[]{:S(2)}) collective-permute-start(f32[8,2048]{1,0:T(8,128)S(1)} %get-tuple-element.147), channel_id=1, source_target_pairs={{0,128},{64,192},{128,0},{192,64},{1,129},{65,193},{129,1},{193,65... | collective-permute-start | bytes 196616 | tf_op jit(solution)/shard_map/ppermute | solution.py:414
  155.2 1.4 collective-permute-start.22
  156.6 0.8 feat_grad.1
  157.3 0.8 collective-permute-done.21.refs_2_
  158.2 1.3 collective-permute-done.22.refs_3_
  159.4 1.3 proto_grad.1
  (105 shorter events, 7.3 us)
Async XLA Ops:
  2.2 12.4 %all-to-all-start = ((f32[4,96,256]{2,1,0:T(8,128)}), f32[4,96,256]{2,1,0:T(8,128)S(1)}, u32[]{:S(2)}, u32[]{:S(2)}) async-start(f32[4,96,256]{2,1,0:T(8,128)} %broadcast_in_dim.2), calls=%async_computation | async-start | bytes 786432 | tf_op jit(solution)/shard_map/all_to_all | solution.py:418
  15.9 16.8 %all-to-all-start.1 = ((f32[8,16,128]{2,1,0:T(8,128)}), f32[8,16,128]{2,1,0:T(8,128)S(1)}, u32[]{:S(2)}, u32[]{:S(2)}) async-start(f32[8,16,128]{2,1,0:T(8,128)} %get-tuple-element.84), calls=%async_computation.1 | async-start | bytes 131072 | tf_op jit(solution)/shard_map/all_to_all | solution.py:418
  24.3 23.2 %collective-permute-start.2 = (f32[248,256]{1,0:T(8,128)S(1)}, f32[248,256]{1,0:T(8,128)S(1)}, u32[]{:S(2)}, u32[]{:S(2)}) collective-permute-start(f32[248,256]{1,0:T(8,128)S(1)} %copy-done.25), channel_id=1, source_target_pairs={{0,128},{64,192},{128,0},{192,64},{1,129},{65,193},{129,1},{193,65... | collective-permute-start | bytes 761864 | tf_op jit(solution)/shard_map/ppermute | solution.py:414
  26.1 21.5 %collective-permute-start.1 = (f32[248,256]{1,0:T(8,128)S(1)}, f32[248,256]{1,0:T(8,128)S(1)}, u32[]{:S(2)}, u32[]{:S(2)}) collective-permute-start(f32[248,256]{1,0:T(8,128)S(1)} %copy-done.25), channel_id=1, source_target_pairs={{0,192},{64,0},{128,64},{192,128},{1,193},{65,1},{129,65},{193,129... | collective-permute-start | bytes 761864 | tf_op jit(solution)/shard_map/ppermute | solution.py:414
  27.7 19.9 %collective-permute-start = (f32[248,256]{1,0:T(8,128)S(1)}, f32[248,256]{1,0:T(8,128)S(1)}, u32[]{:S(2)}, u32[]{:S(2)}) collective-permute-start(f32[248,256]{1,0:T(8,128)S(1)} %copy-done.25), channel_id=1, source_target_pairs={{0,64},{64,128},{128,192},{192,0},{1,65},{65,129},{129,193},{193,1... | collective-permute-start | bytes 761864 | tf_op jit(solution)/shard_map/ppermute | solution.py:414
  34.1 12.8 %all-to-all-start.2 = ((f32[32,8,128]{2,1,0:T(8,128)}), f32[32,8,128]{2,1,0:T(8,128)S(1)}, u32[]{:S(2)}, u32[]{:S(2)}) async-start(f32[32,8,128]{2,1,0:T(8,128)} %row_sums.2), calls=%async_computation.2 | async-start | bytes 262144 | tf_op jit(solution)/shard_map/all_to_all | solution.py:418
  47.6 19.0 %copy-start.22 = (f32[248,256]{1,0:T(8,128)}, f32[248,256]{1,0:T(8,128)S(1)}, u32[]{:S(2)}) copy-start(f32[248,256]{1,0:T(8,128)S(1)} %collective-permute-done.2.mine_2) | copy-start | bytes 761860
  47.6 19.0 %copy-start.23 = (f32[248,256]{1,0:T(8,128)}, f32[248,256]{1,0:T(8,128)S(1)}, u32[]{:S(2)}) copy-start(f32[248,256]{1,0:T(8,128)S(1)} %collective-permute-done.1.mine_3) | copy-start | bytes 761860
  47.6 19.0 %copy-start.24 = (f32[248,256]{1,0:T(8,128)}, f32[248,256]{1,0:T(8,128)S(1)}, u32[]{:S(2)}) copy-start(f32[248,256]{1,0:T(8,128)S(1)} %collective-permute-done.mine_1) | copy-start | bytes 761860
  47.6 12.5 %collective-permute-start.3 = (f32[248,256]{1,0:T(8,128)S(1)}, f32[248,256]{1,0:T(8,128)S(1)}, u32[]{:S(2)}, u32[]{:S(2)}) collective-permute-start(f32[248,256]{1,0:T(8,128)S(1)} %collective-permute-done.mine_1), channel_id=1, source_target_pairs={{0,1},{1,0},{2,3},{3,2},{4,5},{5,4},{6,7},{7,6},{8,9},{9,8},{10,11... | collective-permute-start | bytes 761864 | tf_op jit(solution)/shard_map/ppermute | solution.py:414
  47.8 12.3 %collective-permute-start.5 = (f32[248,256]{1,0:T(8,128)S(1)}, f32[248,256]{1,0:T(8,128)S(1)}, u32[]{:S(2)}, u32[]{:S(2)}) collective-permute-start(f32[248,256]{1,0:T(8,128)S(1)} %collective-permute-done.2.mine_2), channel_id=1, source_target_pairs={{0,1},{1,0},{2,3},{3,2},{4,5},{5,4},{6,7},{7,6},{8,9},{9,8},{10,11... | collective-permute-start | bytes 761864 | tf_op jit(solution)/shard_map/ppermute | solution.py:414
  48.2 11.9 %collective-permute-start.4 = (f32[248,256]{1,0:T(8,128)S(1)}, f32[248,256]{1,0:T(8,128)S(1)}, u32[]{:S(2)}, u32[]{:S(2)}) collective-permute-start(f32[248,256]{1,0:T(8,128)S(1)} %collective-permute-done.1.mine_3), channel_id=1, source_target_pairs={{0,1},{1,0},{2,3},{3,2},{4,5},{5,4},{6,7},{7,6},{8,9},{9,8},{10,11... | collective-permute-start | bytes 761864 | tf_op jit(solution)/shard_map/ppermute | solution.py:414
  61.6 11.7 %all-to-all-start.4 = ((f32[32,8,128]{2,1,0:T(8,128)}), f32[32,8,128]{2,1,0:T(8,128)S(1)}, u32[]{:S(2)}, u32[]{:S(2)}) async-start(f32[32,8,128]{2,1,0:T(8,128)} %row_sums.3), calls=%async_computation.4 | async-start | bytes 262144 | tf_op jit(solution)/shard_map/all_to_all | solution.py:418
  74.6 11.7 %all-to-all-start.5 = ((f32[8,16,128]{2,1,0:T(8,128)}), f32[8,16,128]{2,1,0:T(8,128)S(1)}, u32[]{:S(2)}, u32[]{:S(2)}) async-start(f32[8,16,128]{2,1,0:T(8,128)} %col_sums.3), calls=%async_computation.5 | async-start | bytes 131072 | tf_op jit(solution)/shard_map/all_to_all | solution.py:418
  82.3 20.2 %copy-start.11 = (f32[4,8,512]{2,1,0:T(8,128)S(1)}, f32[4,8,512]{2,1,0:T(8,128)}, u32[]{:S(2)}) copy-start(f32[4,8,512]{2,1,0:T(8,128)} %get-tuple-element.98.crops) | copy-start | bytes 196612
  86.2 16.2 %copy-start.2 = (bf16[256,2048]{1,0:T(8,128)(2,1)S(1)}, bf16[256,2048]{1,0:T(8,128)(2,1)}, u32[]{:S(2)}) copy-start(bf16[256,2048]{1,0:T(8,128)(2,1)} %get-tuple-element.113.tn) | copy-start | bytes 3145732
  86.2 16.2 %copy-start.7 = (bf16[4,256,480]{2,1,0:T(8,128)(2,1)S(1)}, bf16[4,256,480]{2,1,0:T(8,128)(2,1)}, u32[]{:S(2)}) copy-start(bf16[4,256,480]{2,1,0:T(8,128)(2,1)} %get-tuple-element.110.ubt) | copy-start | bytes 2949124
  86.2 16.3 %copy-start.9 = (bf16[1920,256]{1,0:T(8,128)(2,1)S(1)}, bf16[1920,256]{1,0:T(8,128)(2,1)}, u32[]{:S(2)}) copy-start(bf16[1920,256]{1,0:T(8,128)(2,1)} %get-tuple-element.107.ub) | copy-start | bytes 2949124
  86.2 16.3 %copy-start.10 = (bf16[1920,256]{1,0:T(8,128)(2,1)S(1)}, bf16[1920,256]{1,0:T(8,128)(2,1)}, u32[]{:S(2)}) copy-start(bf16[1920,256]{1,0:T(8,128)(2,1)} %get-tuple-element.111.tuc) | copy-start | bytes 2949124
  109.2 11.1 %collective-permute-start.6 = (f32[4,8,1024]{2,1,0:T(8,128)}, f32[4,8,1024]{2,1,0:T(8,128)S(1)}, u32[]{:S(2)}, u32[]{:S(2)}) collective-permute-start(f32[4,8,1024]{2,1,0:T(8,128)} %get-tuple-element.114), channel_id=1, source_target_pairs={{0,8},{8,16},{16,24},{24,32},{32,40},{40,48},{48,56},{56,0},{1,9},... | collective-permute-start | bytes 393224 | tf_op jit(solution)/shard_map/ppermute | solution.py:414
  109.8 10.5 %collective-permute-start.7 = (f32[4,8,1024]{2,1,0:T(8,128)}, f32[4,8,1024]{2,1,0:T(8,128)S(1)}, u32[]{:S(2)}, u32[]{:S(2)}) collective-permute-start(f32[4,8,1024]{2,1,0:T(8,128)} %get-tuple-element.115), channel_id=1, source_target_pairs={{0,56},{8,0},{16,8},{24,16},{32,24},{40,32},{48,40},{56,48},{1,57}... | collective-permute-start | bytes 393224 | tf_op jit(solution)/shard_map/ppermute | solution.py:414
  120.4 12.7 %copy-start.19 = (f32[4,8,1024]{2,1,0:T(8,128)S(1)}, f32[4,8,1024]{2,1,0:T(8,128)}, u32[]{:S(2)}) copy-start(f32[4,8,1024]{2,1,0:T(8,128)} %get-tuple-element.136) | copy-start | bytes 393220
  120.4 13.2 %copy-start.17 = (f32[4,8,1024]{2,1,0:T(8,128)S(1)}, f32[4,8,1024]{2,1,0:T(8,128)}, u32[]{:S(2)}) copy-start(f32[4,8,1024]{2,1,0:T(8,128)} %get-tuple-element.133) | copy-start | bytes 393220
  120.4 15.2 %copy-start.18 = (f32[4,8,1024]{2,1,0:T(8,128)S(1)}, f32[4,8,1024]{2,1,0:T(8,128)}, u32[]{:S(2)}) copy-start(f32[4,8,1024]{2,1,0:T(8,128)} %get-tuple-element.140) | copy-start | bytes 393220
  120.4 17.5 %copy-start.16 = (f32[4,8,1024]{2,1,0:T(8,128)S(1)}, f32[4,8,1024]{2,1,0:T(8,128)}, u32[]{:S(2)}) copy-start(f32[4,8,1024]{2,1,0:T(8,128)} %get-tuple-element.144) | copy-start | bytes 393220
  120.4 36.2 %all-to-all-start.7 = ((f32[32,32,512]{2,1,0:T(8,128)}), f32[32,32,512]{2,1,0:T(8,128)S(1)}, u32[]{:S(2)}, u32[]{:S(2)}) async-start(f32[32,32,512]{2,1,0:T(8,128)} %get-tuple-element.128), calls=%async_computation.7 | async-start | bytes 4194304 | tf_op jit(solution)/shard_map/all_to_all | solution.py:418
  125.7 15.0 %copy-start.15 = (f32[4,8,1024]{2,1,0:T(8,128)S(1)}, f32[4,8,1024]{2,1,0:T(8,128)}, u32[]{:S(2)}) copy-start(f32[4,8,1024]{2,1,0:T(8,128)} %get-tuple-element.137) | copy-start | bytes 393220
  125.8 16.5 %copy-start.13 = (f32[4,8,1024]{2,1,0:T(8,128)S(1)}, f32[4,8,1024]{2,1,0:T(8,128)}, u32[]{:S(2)}) copy-start(f32[4,8,1024]{2,1,0:T(8,128)} %get-tuple-element.134) | copy-start | bytes 393220
  125.8 17.2 %copy-start.14 = (f32[4,8,1024]{2,1,0:T(8,128)S(1)}, f32[4,8,1024]{2,1,0:T(8,128)}, u32[]{:S(2)}) copy-start(f32[4,8,1024]{2,1,0:T(8,128)} %get-tuple-element.141) | copy-start | bytes 393220
  125.8 18.1 %copy-start.12 = (f32[4,8,1024]{2,1,0:T(8,128)S(1)}, f32[4,8,1024]{2,1,0:T(8,128)}, u32[]{:S(2)}) copy-start(f32[4,8,1024]{2,1,0:T(8,128)} %get-tuple-element.145) | copy-start | bytes 393220
  125.8 24.4 %copy-start.5 = (f32[4,8,1024]{2,1,0:T(8,128)S(1)}, f32[4,8,1024]{2,1,0:T(8,128)}, u32[]{:S(2)}) copy-start(f32[4,8,1024]{2,1,0:T(8,128)} %get-tuple-element.130.p0) | copy-start | bytes 393220
  125.8 24.4 %copy-start.6 = (f32[4,8,1024]{2,1,0:T(8,128)S(1)}, f32[4,8,1024]{2,1,0:T(8,128)}, u32[]{:S(2)}) copy-start(f32[4,8,1024]{2,1,0:T(8,128)} %get-tuple-element.138.p1) | copy-start | bytes 393220
  125.8 5.6 %collective-permute-start.16 = (f32[4,8,1024]{2,1,0:T(8,128)S(1)}, f32[4,8,1024]{2,1,0:T(8,128)S(1)}, u32[]{:S(2)}, u32[]{:S(2)}) collective-permute-start(f32[4,8,1024]{2,1,0:T(8,128)S(1)} %copy-done.30), channel_id=1, source_target_pairs={{0,56},{8,0},{16,8},{24,16},{32,24},{40,32},{48,40},{56,48},{1,57}... | collective-permute-start | bytes 393224 | tf_op jit(solution)/shard_map/ppermute | solution.py:414
  125.9 7.6 %collective-permute-start.8 = (f32[4,8,1024]{2,1,0:T(8,128)S(1)}, f32[4,8,1024]{2,1,0:T(8,128)S(1)}, u32[]{:S(2)}, u32[]{:S(2)}) collective-permute-start(f32[4,8,1024]{2,1,0:T(8,128)S(1)} %add.32), channel_id=1, source_target_pairs={{0,8},{8,16},{16,24},{24,32},{32,40},{40,48},{48,56},{56,0},{1,9},... | collective-permute-start | bytes 393224 | tf_op jit(solution)/shard_map/ppermute | solution.py:414
  128.0 7.6 %collective-permute-start.13 = (f32[4,8,1024]{2,1,0:T(8,128)S(1)}, f32[4,8,1024]{2,1,0:T(8,128)S(1)}, u32[]{:S(2)}, u32[]{:S(2)}) collective-permute-start(f32[4,8,1024]{2,1,0:T(8,128)S(1)} %copy-done.29), channel_id=1, source_target_pairs={{0,8},{8,16},{16,24},{24,32},{32,40},{40,48},{48,56},{56,0},{1,9},... | collective-permute-start | bytes 393224 | tf_op jit(solution)/shard_map/ppermute | solution.py:414
  131.5 6.4 %collective-permute-start.17 = (f32[4,8,1024]{2,1,0:T(8,128)S(1)}, f32[4,8,1024]{2,1,0:T(8,128)S(1)}, u32[]{:S(2)}, u32[]{:S(2)}) collective-permute-start(f32[4,8,1024]{2,1,0:T(8,128)S(1)} %add.39), channel_id=1, source_target_pairs={{0,56},{8,0},{16,8},{24,16},{32,24},{40,32},{48,40},{56,48},{1,57}... | collective-permute-start | bytes 393224 | tf_op jit(solution)/shard_map/ppermute | solution.py:414
  133.1 7.7 %collective-permute-start.11 = (f32[4,8,1024]{2,1,0:T(8,128)S(1)}, f32[4,8,1024]{2,1,0:T(8,128)S(1)}, u32[]{:S(2)}, u32[]{:S(2)}) collective-permute-start(f32[4,8,1024]{2,1,0:T(8,128)S(1)} %add.35), channel_id=1, source_target_pairs={{0,56},{8,0},{16,8},{24,16},{32,24},{40,32},{48,40},{56,48},{1,57}... | collective-permute-start | bytes 393224 | tf_op jit(solution)/shard_map/ppermute | solution.py:414
  133.6 8.7 %collective-permute-start.9 = (f32[4,8,1024]{2,1,0:T(8,128)S(1)}, f32[4,8,1024]{2,1,0:T(8,128)S(1)}, u32[]{:S(2)}, u32[]{:S(2)}) collective-permute-start(f32[4,8,1024]{2,1,0:T(8,128)S(1)} %add.33), channel_id=1, source_target_pairs={{0,8},{8,16},{16,24},{24,32},{32,40},{40,48},{48,56},{56,0},{1,9},... | collective-permute-start | bytes 393224 | tf_op jit(solution)/shard_map/ppermute | solution.py:414
  135.6 7.4 %collective-permute-start.14 = (f32[4,8,1024]{2,1,0:T(8,128)S(1)}, f32[4,8,1024]{2,1,0:T(8,128)S(1)}, u32[]{:S(2)}, u32[]{:S(2)}) collective-permute-start(f32[4,8,1024]{2,1,0:T(8,128)S(1)} %add.37), channel_id=1, source_target_pairs={{0,8},{8,16},{16,24},{24,32},{32,40},{40,48},{48,56},{56,0},{1,9},... | collective-permute-start | bytes 393224 | tf_op jit(solution)/shard_map/ppermute | solution.py:414
  137.9 5.9 %collective-permute-start.18 = (f32[4,8,1024]{2,1,0:T(8,128)S(1)}, f32[4,8,1024]{2,1,0:T(8,128)S(1)}, u32[]{:S(2)}, u32[]{:S(2)}) collective-permute-start(f32[4,8,1024]{2,1,0:T(8,128)S(1)} %add.40), channel_id=1, source_target_pairs={{0,56},{8,0},{16,8},{24,16},{32,24},{40,32},{48,40},{56,48},{1,57}... | collective-permute-start | bytes 393224 | tf_op jit(solution)/shard_map/ppermute | solution.py:414
  140.8 6.9 %collective-permute-start.12 = (f32[4,8,1024]{2,1,0:T(8,128)S(1)}, f32[4,8,1024]{2,1,0:T(8,128)S(1)}, u32[]{:S(2)}, u32[]{:S(2)}) collective-permute-start(f32[4,8,1024]{2,1,0:T(8,128)S(1)} %add.36), channel_id=1, source_target_pairs={{0,56},{8,0},{16,8},{24,16},{32,24},{40,32},{48,40},{56,48},{1,57}... | collective-permute-start | bytes 393224 | tf_op jit(solution)/shard_map/ppermute | solution.py:414
  142.3 6.5 %collective-permute-start.10 = (f32[4,8,1024]{2,1,0:T(8,128)S(1)}, f32[4,8,1024]{2,1,0:T(8,128)S(1)}, u32[]{:S(2)}, u32[]{:S(2)}) collective-permute-start(f32[4,8,1024]{2,1,0:T(8,128)S(1)} %add.34), channel_id=1, source_target_pairs={{0,8},{8,16},{16,24},{24,32},{32,40},{40,48},{48,56},{56,0},{1,9},... | collective-permute-start | bytes 393224 | tf_op jit(solution)/shard_map/ppermute | solution.py:414
  143.0 13.6 %copy-start.3 = (f32[40,480]{1,0:T(8,128)S(1)}, f32[40,480]{1,0:T(8,128)}, u32[]{:S(2)}) copy-start(f32[40,480]{1,0:T(8,128)} %get-tuple-element.129.mine) | copy-start | bytes 230404
  143.0 7.2 %collective-permute-start.15 = (f32[4,8,1024]{2,1,0:T(8,128)S(1)}, f32[4,8,1024]{2,1,0:T(8,128)S(1)}, u32[]{:S(2)}, u32[]{:S(2)}) collective-permute-start(f32[4,8,1024]{2,1,0:T(8,128)S(1)} %add.38), channel_id=1, source_target_pairs={{0,8},{8,16},{16,24},{24,32},{32,40},{40,48},{48,56},{56,0},{1,9},... | collective-permute-start | bytes 393224 | tf_op jit(solution)/shard_map/ppermute | solution.py:414
  143.9 6.3 %collective-permute-start.19 = (f32[4,8,1024]{2,1,0:T(8,128)S(1)}, f32[4,8,1024]{2,1,0:T(8,128)S(1)}, u32[]{:S(2)}, u32[]{:S(2)}) collective-permute-start(f32[4,8,1024]{2,1,0:T(8,128)S(1)} %add.41), channel_id=1, source_target_pairs={{0,56},{8,0},{16,8},{24,16},{32,24},{40,32},{48,40},{56,48},{1,57}... | collective-permute-start | bytes 393224 | tf_op jit(solution)/shard_map/ppermute | solution.py:414
  150.8 6.5 %collective-permute-start.20 = (f32[8,2048]{1,0:T(8,128)S(1)}, f32[8,2048]{1,0:T(8,128)S(1)}, u32[]{:S(2)}, u32[]{:S(2)}) collective-permute-start(f32[8,2048]{1,0:T(8,128)S(1)} %get-tuple-element.146), channel_id=1, source_target_pairs={{0,64},{64,128},{128,192},{192,0},{1,65},{65,129},{129,193},{193,1... | collective-permute-start | bytes 196616 | tf_op jit(solution)/shard_map/ppermute | solution.py:414
  152.4 5.8 %collective-permute-start.21 = (f32[8,2048]{1,0:T(8,128)S(1)}, f32[8,2048]{1,0:T(8,128)S(1)}, u32[]{:S(2)}, u32[]{:S(2)}) collective-permute-start(f32[8,2048]{1,0:T(8,128)S(1)} %get-tuple-element.147), channel_id=1, source_target_pairs={{0,128},{64,192},{128,0},{192,64},{1,129},{65,193},{129,1},{193,65... | collective-permute-start | bytes 196616 | tf_op jit(solution)/shard_map/ppermute | solution.py:414
  155.2 4.3 %collective-permute-start.22 = (f32[8,2048]{1,0:T(8,128)S(1)}, f32[8,2048]{1,0:T(8,128)S(1)}, u32[]{:S(2)}, u32[]{:S(2)}) collective-permute-start(f32[8,2048]{1,0:T(8,128)S(1)} %get-tuple-element.148), channel_id=1, source_target_pairs={{0,192},{64,0},{128,64},{192,128},{1,193},{65,1},{129,65},{193,129... | collective-permute-start | bytes 196616 | tf_op jit(solution)/shard_map/ppermute | solution.py:414
  (12 other events, 78.2 us)

commit v2 on v1

--- a/solution.py
+++ b/solution.py
@@ -330,7 +330,7 @@
         out(x).wait()
 
 
-def grad_call(kernel, outs, specs, name, scratch, at, *args):
+def grad_call(kernel, outs, specs, first, name, scratch, at, *args):
     whole = lambda v: pl.BlockSpec(v.shape, lambda i, at, n=len(v.shape): (0,) * n)
     return pl.pallas_call(
         kernel,
@@ -341,7 +341,10 @@
             out_specs=[whole(arr(NX, 8, HALF))] * NZ + (specs or [whole(v) for v in outs]),
             scratch_shapes=[pltpu.VMEM((K, HALF), f32)] + scratch,
         ),
-        out_shape=[pltpu.HBM((NX, 8, HALF), f32)] * NZ + outs,
+        out_shape=[
+            arr(NX, 8, HALF) if d in first else pltpu.HBM((NX, 8, HALF), f32) for d in range(NZ)
+        ]
+        + outs,
         cost_estimate=cost(8),
         compiler_params=pltpu.CompilerParams(vmem_limit_bytes=GRAD_MIB * MIB),
         name=name,
@@ -350,14 +353,14 @@
 
 def first_pass(at, crops, parts, *common):
     outs = [arr(SROWS, K), arr(SROWS, 128)]
-    *p, g, coef = grad_call(first_kernel, outs, None, "first_half", [], at, crops, parts, *common)
+    *p, g, coef = grad_call(first_kernel, outs, None, (4, 5), "first_half", [], at, crops, parts, *common)
     return p, g, coef
 
 
 def second_pass(at, coef, g, ut, *common):
     outs, specs = [pltpu.HBM((NROW, 32, 512), f32)], [pl.BlockSpec(memory_space=pltpu.HBM)]
     scratch = [pltpu.VMEM((NX, NY * NC, 32, 512), f32), pltpu.SemaphoreType.DMA((NX,))]
-    *p, g = grad_call(second_kernel, outs, specs, "second_half", scratch, at, coef, g, ut, *common)
+    *p, g = grad_call(second_kernel, outs, specs, (3, 4), "second_half", scratch, at, coef, g, ut, *common)
     return p, g
 
 

time: 162 us -> 162 us (level)
  starting transfers between devices: 61.3 us -> 59.3 us
    ppermute x23, starting transfers between devices: 28.6 us -> 26.8 us  [shift(): return lax.ppermute(v, axis, [(i, (i + d) % size) for i in range(size)])]
  transfers between devices with their start and end apart: 29 -> 29, of which waited for: 14 -> 15; matrix products, arithmetic and copies ran while one was open for 1% -> 1% of each run, Pallas kernels for 17% -> 17%
where the time goes in v2:
time: 162 us
  starting transfers between devices  59.3 us (37%)
  Pallas kernels  39.9 us (25%)
  waiting for transfers between devices  27.4 us (17%)
  blocking collectives  27.3 us (17%)
  local copies, waits for them, and re-layouts  4.53 us (3%)
  other arithmetic  2.01 us (1%)
    all_to_all x6, starting transfers between devices, exchange(): return lax.all_to_all(v, axes, 0, 0, tiled=False)  32.5 us
    all_to_all x2, blocking collectives, exchange(): return lax.all_to_all(v, axes, 0, 0, tiled=False)  27.3 us
    ppermute x23, starting transfers between devices, shift(): return lax.ppermute(v, axis, [(i, (i + d) % size) for i in range(size)])  26.8 us
    all_to_all x6, waiting for transfers between devices, exchange(): return lax.all_to_all(v, axes, 0, 0, tiled=False)  14.9 us
    pallas_call x2, Pallas kernels, grad_call(): pl.pallas_call(kernel, grid_spec=pltpu.PrefetchScalarGridSpec(num_scalar_...  14.3 us
    ppermute x23, waiting for transfers between devices, shift(): return lax.ppermute(v, axis, [(i, (i + d) % size) for i in range(size)])  12.5 us
    pallas_call x1, Pallas kernels, rows_pass(): pl.pallas_call(rows_kernel, grid_spec=pltpu.PrefetchScalarGridSpec(num_sc...  5.87 us
    pallas_call x2, Pallas kernels, norm_pass(): pl.pallas_call(norm_kernel, grid_spec=pltpu.PrefetchScalarGridSpec(num_sc...  5.82 us
  transfers between devices with their start and end apart: 29, of which 15 were waited for; matrix products, arithmetic and copies ran while one was open for 1% of the time, Pallas kernels for 17%

profile of v2, /device:TPU:8, one launch (start us, length us, event | category | flops | bytes accessed | tf_op | source)
XLA Modules:
  0.0 161.6 jit_solution(4862858314282626900)
XLA Ops:
  0.6 1.6 broadcast_in_dim.2
  2.2 4.3 %all-to-all-start = ((f32[4,96,256]{2,1,0:T(8,128)}), f32[4,96,256]{2,1,0:T(8,128)S(1)}, u32[]{:S(2)}, u32[]{:S(2)}) async-start(f32[4,96,256]{2,1,0:T(8,128)} %broadcast_in_dim.2), calls=%async_computation | async-start | bytes 786432 | tf_op jit(solution)/shard_map/all_to_all | solution.py:421
  7.4 0.9 copy-done
  8.3 1.4 pack_rows.1
  9.8 3.0 %teacher_norm.1 = (bf16[256,2048]{1,0:T(8,128)(2,1)}, bf16[256,2048]{1,0:T(8,128)(2,1)S(1)}) custom-call(s32[4]{0:T(128)S(1)} %pad_add_fusion.at, bf16[256,8192]{1,0:T(8,128)(2,1)} %w.2), custom_call_target="tpu_custom_call" | custom-call | flops 2000000000 | tf_op jit(solution)/shard_map/teacher_norm/pallas_call | solution.py:88
  12.8 1.8 %all-to-all-done.tf = f32[4,96,256]{2,1,0:T(8,128)S(1)} async-done(((f32[4,96,256]{2,1,0:T(8,128)}), f32[4,96,256]{2,1,0:T(8,128)S(1)}, u32[]{:S(2)}, u32[]{:S(2)}) %all-to-all-start) | async-done | bytes 393248 | tf_op jit(solution)/shard_map/all_to_all | solution.py:421
  14.6 1.3 teacher_scores.1
  15.9 8.5 %all-to-all-start.1 = ((f32[8,16,128]{2,1,0:T(8,128)}), f32[8,16,128]{2,1,0:T(8,128)S(1)}, u32[]{:S(2)}, u32[]{:S(2)}) async-start(f32[8,16,128]{2,1,0:T(8,128)} %get-tuple-element.84), calls=%async_computation.1 | async-start | bytes 131072 | tf_op jit(solution)/shard_map/all_to_all | solution.py:421
  24.4 1.8 %collective-permute-start.2 = (f32[248,256]{1,0:T(8,128)S(1)}, f32[248,256]{1,0:T(8,128)S(1)}, u32[]{:S(2)}, u32[]{:S(2)}) collective-permute-start(f32[248,256]{1,0:T(8,128)S(1)} %copy-done.26), channel_id=1, source_target_pairs={{0,128},{64,192},{128,0},{192,64},{1,129},{65,193},{129,1},{193,65... | collective-permute-start | bytes 761864 | tf_op jit(solution)/shard_map/ppermute | solution.py:417
  26.1 1.5 collective-permute-start.1
  28.2 4.6 %all-to-all-done.1.c_parts = f32[8,16,128]{2,1,0:T(8,128)S(1)} async-done(((f32[8,16,128]{2,1,0:T(8,128)}), f32[8,16,128]{2,1,0:T(8,128)S(1)}, u32[]{:S(2)}, u32[]{:S(2)}) %all-to-all-start.1) | async-done | bytes 65568 | tf_op jit(solution)/shard_map/all_to_all | solution.py:421
  32.7 1.4 row_sums.2
  34.1 6.2 %all-to-all-start.2 = ((f32[32,8,128]{2,1,0:T(8,128)}), f32[32,8,128]{2,1,0:T(8,128)S(1)}, u32[]{:S(2)}, u32[]{:S(2)}) async-start(f32[32,8,128]{2,1,0:T(8,128)} %row_sums.2), calls=%async_computation.2 | async-start | bytes 262144 | tf_op jit(solution)/shard_map/all_to_all | solution.py:421
  40.3 2.8 %student_norm.1.sn = bf16[256,2048]{1,0:T(8,128)(2,1)} custom-call(s32[4]{0:T(128)S(1)} %pad_add_fusion.at, bf16[256,8192]{1,0:T(8,128)(2,1)} %w.3), custom_call_target="tpu_custom_call" | custom-call | flops 2000000000 | tf_op jit(solution)/shard_map/student_norm/pallas_call | solution.py:88
  43.1 3.8 %all-to-all-done.2.r_parts = f32[32,8,128]{2,1,0:T(8,128)S(1)} async-done(((f32[32,8,128]{2,1,0:T(8,128)}), f32[32,8,128]{2,1,0:T(8,128)S(1)}, u32[]{:S(2)}, u32[]{:S(2)}) %all-to-all-start.2) | async-done | bytes 131104 | tf_op jit(solution)/shard_map/all_to_all | solution.py:421
  48.4 11.8 %all_to_all.40.c_parts = f32[8,16,128]{2,1,0:T(8,128)S(1)} all-to-all(f32[8,16,128]{2,1,0:T(8,128)S(1)} %col_sums.2), channel_id=1, replica_groups=mesh['x'=4,'z'=8,'y'=4,'c'=2] {'z'}, dimensions={0} | all-to-all | bytes 131072 | tf_op jit(solution)/shard_map/all_to_all | solution.py:421
  60.2 1.4 row_sums.3
  61.5 5.0 %all-to-all-start.4 = ((f32[32,8,128]{2,1,0:T(8,128)}), f32[32,8,128]{2,1,0:T(8,128)S(1)}, u32[]{:S(2)}, u32[]{:S(2)}) async-start(f32[32,8,128]{2,1,0:T(8,128)} %row_sums.3), calls=%async_computation.4 | async-start | bytes 262144 | tf_op jit(solution)/shard_map/all_to_all | solution.py:421
  66.6 5.9 %student_units.1 = (bf16[1920,256]{1,0:T(8,128)(2,1)}, bf16[4,256,480]{2,1,0:T(8,128)(2,1)}, f32[4,256,480]{2,1,0:T(8,128)}, bf16[1920,256]{1,0:T(8,128)(2,1)}, f32[4,8,512]{2,1,0:T(8,128)}, /*index=5*/f32[40,480]{1,0:T(8,128)}) custom-call(s32[4]{0:T(128)S(1)} %pad_add_fusion.at, f32[488,256]{1,0:T(8,128)} %get-tuple-element.81.own, f32[248,256]{1,0:T(8,128)} %copy-done.25, ...), custom_call_target="tpu_custom_call" | custom-call | flops 3000000000 | tf_op jit(solution)/shard_map/student_units/pallas_call | solution.py:225
  72.5 0.8 all-to-all-done.4.r_parts
  73.3 1.3 col_sums.3
  74.6 3.4 %all-to-all-start.5 = ((f32[8,16,128]{2,1,0:T(8,128)}), f32[8,16,128]{2,1,0:T(8,128)S(1)}, u32[]{:S(2)}, u32[]{:S(2)}) async-start(f32[8,16,128]{2,1,0:T(8,128)} %col_sums.3), calls=%async_computation.5 | async-start | bytes 131072 | tf_op jit(solution)/shard_map/all_to_all | solution.py:421
  77.9 1.2 copy-done.8
  79.1 3.1 %student_sums.1.refs_0_ = f32[16,128]{1,0:T(8,128)S(1)} custom-call(bf16[1920,256]{1,0:T(8,128)(2,1)S(1)} %copy-done.8, bf16[256,2048]{1,0:T(8,128)(2,1)S(1)} %copy-done.1), custom_call_target="tpu_custom_call" | custom-call | flops 3000000000 | tf_op jit(solution)/shard_map/student_sums/pallas_call | solution.py:260
  82.3 4.0 %all-to-all-done.5.c_parts = f32[8,16,128]{2,1,0:T(8,128)S(1)} async-done(((f32[8,16,128]{2,1,0:T(8,128)}), f32[8,16,128]{2,1,0:T(8,128)S(1)}, u32[]{:S(2)}, u32[]{:S(2)}) %all-to-all-start.5) | async-done | bytes 65568 | tf_op jit(solution)/shard_map/all_to_all | solution.py:421
  86.9 15.5 %all_to_all.41.parts = f32[32,24,128]{2,1,0:T(8,128)S(1)} all-to-all(f32[32,24,128]{2,1,0:T(8,128)S(1)} %get-tuple-element.109), channel_id=1, replica_groups=mesh['x'=4,'z'=8,'y'=4,'c'=2] {'x','y','c'}, dimensions={0} | all-to-all | bytes 786432 | tf_op jit(solution)/shard_map/all_to_all | solution.py:421
  102.5 6.6 %first_half.1 = (f32[4,8,1024]{2,1,0:T(8,128)}, f32[4,8,1024]{2,1,0:T(8,128)}, f32[4,8,1024]{2,1,0:T(8,128)}, f32[4,8,1024]{2,1,0:T(8,128)}, f32[4,8,1024]{2,1,0...) custom-call(s32[4]{0:T(128)S(1)} %pad_add_fusion.at, ...), custom_call_target="tpu_custom_call" | custom-call | flops 8000000000 | tf_op jit(solution)/shard_map/first_half/pallas_call | solution.py:335
  109.7 2.7 %collective-permute-start.7 = (f32[4,8,1024]{2,1,0:T(8,128)S(1)}, f32[4,8,1024]{2,1,0:T(8,128)S(1)}, u32[]{:S(2)}, u32[]{:S(2)}) collective-permute-start(f32[4,8,1024]{2,1,0:T(8,128)S(1)} %get-tuple-element.115), channel_id=1, source_target_pairs={{0,56},{8,0},{16,8},{24,16},{32,24},{40,32},{48,40},{56,48},{1,57}... | collective-permute-start | bytes 393224 | tf_op jit(solution)/shard_map/ppermute | solution.py:417
  112.4 7.7 %second_half.1 = (f32[4,8,1024]{2,1,0:T(8,128)}, f32[4,8,1024]{2,1,0:T(8,128)}, f32[4,8,1024]{2,1,0:T(8,128)}, f32[4,8,1024]{2,1,0:T(8,128)S(1)}, f32[4,8,1024]{...) custom-call(s32[4]{0:T(128)S(1)} %pad_add_fusion.at, ...), custom_call_target="tpu_custom_call" | custom-call | flops 8000000000 | tf_op jit(solution)/shard_map/second_half/pallas_call | solution.py:335
  120.8 5.2 %all-to-all-start.7 = ((f32[32,32,512]{2,1,0:T(8,128)}), f32[32,32,512]{2,1,0:T(8,128)S(1)}, u32[]{:S(2)}, u32[]{:S(2)}) async-start(f32[32,32,512]{2,1,0:T(8,128)} %get-tuple-element.128), calls=%async_computation.7 | async-start | bytes 4194304 | tf_op jit(solution)/shard_map/all_to_all | solution.py:421
  126.1 1.1 add.32
  127.2 1.9 %collective-permute-start.8 = (f32[4,8,1024]{2,1,0:T(8,128)S(1)}, f32[4,8,1024]{2,1,0:T(8,128)S(1)}, u32[]{:S(2)}, u32[]{:S(2)}) collective-permute-start(f32[4,8,1024]{2,1,0:T(8,128)S(1)} %add.32), channel_id=1, source_target_pairs={{0,8},{8,16},{16,24},{24,32},{32,40},{40,48},{48,56},{56,0},{1,9},... | collective-permute-start | bytes 393224 | tf_op jit(solution)/shard_map/ppermute | solution.py:417
  129.2 2.4 %collective-permute-done.16 = f32[4,8,1024]{2,1,0:T(8,128)S(1)} collective-permute-done((f32[4,8,1024]{2,1,0:T(8,128)S(1)}, f32[4,8,1024]{2,1,0:T(8,128)S(1)}, u32[]{:S(2)}, u32[]{:S(2)}) %collective-permute-start.16) | collective-permute-done | bytes 131104 | tf_op jit(solution)/shard_map/ppermute | solution.py:417
  131.7 1.6 collective-permute-start.17
  133.4 1.5 collective-permute-done.8
  135.6 1.3 collective-permute-done.13
  137.3 0.8 collective-permute-done.17
  138.1 2.8 %collective-permute-start.18 = (f32[4,8,1024]{2,1,0:T(8,128)S(1)}, f32[4,8,1024]{2,1,0:T(8,128)S(1)}, u32[]{:S(2)}, u32[]{:S(2)}) collective-permute-start(f32[4,8,1024]{2,1,0:T(8,128)S(1)} %add.40), channel_id=1, source_target_pairs={{0,56},{8,0},{16,8},{24,16},{32,24},{40,32},{48,40},{56,48},{1,57}... | collective-permute-start | bytes 393224 | tf_op jit(solution)/shard_map/ppermute | solution.py:417
  141.0 1.4 collective-permute-start.12
  144.6 3.3 %collective-permute-start.19 = (f32[4,8,1024]{2,1,0:T(8,128)S(1)}, f32[4,8,1024]{2,1,0:T(8,128)S(1)}, u32[]{:S(2)}, u32[]{:S(2)}) collective-permute-start(f32[4,8,1024]{2,1,0:T(8,128)S(1)} %add.41), channel_id=1, source_target_pairs={{0,56},{8,0},{16,8},{24,16},{32,24},{40,32},{48,40},{56,48},{1,57}... | collective-permute-start | bytes 393224 | tf_op jit(solution)/shard_map/ppermute | solution.py:417
  147.9 1.8 %collective-permute-done.10.u0 = f32[4,8,1024]{2,1,0:T(8,128)S(1)} collective-permute-done((f32[4,8,1024]{2,1,0:T(8,128)S(1)}, f32[4,8,1024]{2,1,0:T(8,128)S(1)}, u32[]{:S(2)}, u32[]{:S(2)}) %collective-permute-start.10) | collective-permute-done | bytes 131104 | tf_op jit(solution)/shard_map/ppermute | solution.py:417
  149.6 1.4 collective-permute-done.15.u1
  151.6 1.6 collective-permute-start.20
  153.2 2.8 %collective-permute-start.21 = (f32[8,2048]{1,0:T(8,128)S(1)}, f32[8,2048]{1,0:T(8,128)S(1)}, u32[]{:S(2)}, u32[]{:S(2)}) collective-permute-start(f32[8,2048]{1,0:T(8,128)S(1)} %get-tuple-element.147), channel_id=1, source_target_pairs={{0,128},{64,192},{128,0},{192,64},{1,129},{65,193},{129,1},{193,65... | collective-permute-start | bytes 196616 | tf_op jit(solution)/shard_map/ppermute | solution.py:417
  156.0 1.4 collective-permute-start.22
  158.2 0.8 collective-permute-done.21.refs_2_
  159.0 1.3 collective-permute-done.22.refs_3_
  160.3 1.3 proto_grad.1
  (103 shorter events, 9.8 us)
Async XLA Ops:
  2.2 12.4 %all-to-all-start = ((f32[4,96,256]{2,1,0:T(8,128)}), f32[4,96,256]{2,1,0:T(8,128)S(1)}, u32[]{:S(2)}, u32[]{:S(2)}) async-start(f32[4,96,256]{2,1,0:T(8,128)} %broadcast_in_dim.2), calls=%async_computation | async-start | bytes 786432 | tf_op jit(solution)/shard_map/all_to_all | solution.py:421
  15.9 16.8 %all-to-all-start.1 = ((f32[8,16,128]{2,1,0:T(8,128)}), f32[8,16,128]{2,1,0:T(8,128)S(1)}, u32[]{:S(2)}, u32[]{:S(2)}) async-start(f32[8,16,128]{2,1,0:T(8,128)} %get-tuple-element.84), calls=%async_computation.1 | async-start | bytes 131072 | tf_op jit(solution)/shard_map/all_to_all | solution.py:421
  24.4 23.2 %collective-permute-start.2 = (f32[248,256]{1,0:T(8,128)S(1)}, f32[248,256]{1,0:T(8,128)S(1)}, u32[]{:S(2)}, u32[]{:S(2)}) collective-permute-start(f32[248,256]{1,0:T(8,128)S(1)} %copy-done.26), channel_id=1, source_target_pairs={{0,128},{64,192},{128,0},{192,64},{1,129},{65,193},{129,1},{193,65... | collective-permute-start | bytes 761864 | tf_op jit(solution)/shard_map/ppermute | solution.py:417
  26.1 21.5 %collective-permute-start.1 = (f32[248,256]{1,0:T(8,128)S(1)}, f32[248,256]{1,0:T(8,128)S(1)}, u32[]{:S(2)}, u32[]{:S(2)}) collective-permute-start(f32[248,256]{1,0:T(8,128)S(1)} %copy-done.26), channel_id=1, source_target_pairs={{0,192},{64,0},{128,64},{192,128},{1,193},{65,1},{129,65},{193,129... | collective-permute-start | bytes 761864 | tf_op jit(solution)/shard_map/ppermute | solution.py:417
  27.7 20.0 %collective-permute-start = (f32[248,256]{1,0:T(8,128)S(1)}, f32[248,256]{1,0:T(8,128)S(1)}, u32[]{:S(2)}, u32[]{:S(2)}) collective-permute-start(f32[248,256]{1,0:T(8,128)S(1)} %copy-done.26), channel_id=1, source_target_pairs={{0,64},{64,128},{128,192},{192,0},{1,65},{65,129},{129,193},{193,1... | collective-permute-start | bytes 761864 | tf_op jit(solution)/shard_map/ppermute | solution.py:417
  34.1 12.8 %all-to-all-start.2 = ((f32[32,8,128]{2,1,0:T(8,128)}), f32[32,8,128]{2,1,0:T(8,128)S(1)}, u32[]{:S(2)}, u32[]{:S(2)}) async-start(f32[32,8,128]{2,1,0:T(8,128)} %row_sums.2), calls=%async_computation.2 | async-start | bytes 262144 | tf_op jit(solution)/shard_map/all_to_all | solution.py:421
  47.6 19.0 %copy-start.23 = (f32[248,256]{1,0:T(8,128)}, f32[248,256]{1,0:T(8,128)S(1)}, u32[]{:S(2)}) copy-start(f32[248,256]{1,0:T(8,128)S(1)} %collective-permute-done.2.mine_2) | copy-start | bytes 761860
  47.6 18.9 %copy-start.24 = (f32[248,256]{1,0:T(8,128)}, f32[248,256]{1,0:T(8,128)S(1)}, u32[]{:S(2)}) copy-start(f32[248,256]{1,0:T(8,128)S(1)} %collective-permute-done.1.mine_3) | copy-start | bytes 761860
  47.6 18.9 %copy-start.25 = (f32[248,256]{1,0:T(8,128)}, f32[248,256]{1,0:T(8,128)S(1)}, u32[]{:S(2)}) copy-start(f32[248,256]{1,0:T(8,128)S(1)} %collective-permute-done.mine_1) | copy-start | bytes 761860
  47.7 12.5 %collective-permute-start.3 = (f32[248,256]{1,0:T(8,128)S(1)}, f32[248,256]{1,0:T(8,128)S(1)}, u32[]{:S(2)}, u32[]{:S(2)}) collective-permute-start(f32[248,256]{1,0:T(8,128)S(1)} %collective-permute-done.mine_1), channel_id=1, source_target_pairs={{0,1},{1,0},{2,3},{3,2},{4,5},{5,4},{6,7},{7,6},{8,9},{9,8},{10,11... | collective-permute-start | bytes 761864 | tf_op jit(solution)/shard_map/ppermute | solution.py:417
  47.8 12.3 %collective-permute-start.5 = (f32[248,256]{1,0:T(8,128)S(1)}, f32[248,256]{1,0:T(8,128)S(1)}, u32[]{:S(2)}, u32[]{:S(2)}) collective-permute-start(f32[248,256]{1,0:T(8,128)S(1)} %collective-permute-done.2.mine_2), channel_id=1, source_target_pairs={{0,1},{1,0},{2,3},{3,2},{4,5},{5,4},{6,7},{7,6},{8,9},{9,8},{10,11... | collective-permute-start | bytes 761864 | tf_op jit(solution)/shard_map/ppermute | solution.py:417
  48.2 11.9 %collective-permute-start.4 = (f32[248,256]{1,0:T(8,128)S(1)}, f32[248,256]{1,0:T(8,128)S(1)}, u32[]{:S(2)}, u32[]{:S(2)}) collective-permute-start(f32[248,256]{1,0:T(8,128)S(1)} %collective-permute-done.1.mine_3), channel_id=1, source_target_pairs={{0,1},{1,0},{2,3},{3,2},{4,5},{5,4},{6,7},{7,6},{8,9},{9,8},{10,11... | collective-permute-start | bytes 761864 | tf_op jit(solution)/shard_map/ppermute | solution.py:417
  61.5 11.7 %all-to-all-start.4 = ((f32[32,8,128]{2,1,0:T(8,128)}), f32[32,8,128]{2,1,0:T(8,128)S(1)}, u32[]{:S(2)}, u32[]{:S(2)}) async-start(f32[32,8,128]{2,1,0:T(8,128)} %row_sums.3), calls=%async_computation.4 | async-start | bytes 262144 | tf_op jit(solution)/shard_map/all_to_all | solution.py:421
  74.6 11.7 %all-to-all-start.5 = ((f32[8,16,128]{2,1,0:T(8,128)}), f32[8,16,128]{2,1,0:T(8,128)S(1)}, u32[]{:S(2)}, u32[]{:S(2)}) async-start(f32[8,16,128]{2,1,0:T(8,128)} %col_sums.3), calls=%async_computation.5 | async-start | bytes 131072 | tf_op jit(solution)/shard_map/all_to_all | solution.py:421
  82.2 20.2 %copy-start.11 = (f32[4,8,512]{2,1,0:T(8,128)S(1)}, f32[4,8,512]{2,1,0:T(8,128)}, u32[]{:S(2)}) copy-start(f32[4,8,512]{2,1,0:T(8,128)} %get-tuple-element.98.crops) | copy-start | bytes 196612
  86.2 16.3 %copy-start.2 = (bf16[256,2048]{1,0:T(8,128)(2,1)S(1)}, bf16[256,2048]{1,0:T(8,128)(2,1)}, u32[]{:S(2)}) copy-start(bf16[256,2048]{1,0:T(8,128)(2,1)} %get-tuple-element.113.tn) | copy-start | bytes 3145732
  86.2 16.3 %copy-start.7 = (bf16[4,256,480]{2,1,0:T(8,128)(2,1)S(1)}, bf16[4,256,480]{2,1,0:T(8,128)(2,1)}, u32[]{:S(2)}) copy-start(bf16[4,256,480]{2,1,0:T(8,128)(2,1)} %get-tuple-element.110.ubt) | copy-start | bytes 2949124
  86.2 16.3 %copy-start.9 = (bf16[1920,256]{1,0:T(8,128)(2,1)S(1)}, bf16[1920,256]{1,0:T(8,128)(2,1)}, u32[]{:S(2)}) copy-start(bf16[1920,256]{1,0:T(8,128)(2,1)} %get-tuple-element.107.ub) | copy-start | bytes 2949124
  86.2 16.3 %copy-start.10 = (bf16[1920,256]{1,0:T(8,128)(2,1)S(1)}, bf16[1920,256]{1,0:T(8,128)(2,1)}, u32[]{:S(2)}) copy-start(bf16[1920,256]{1,0:T(8,128)(2,1)} %get-tuple-element.111.tuc) | copy-start | bytes 2949124
  109.1 11.0 %collective-permute-start.6 = (f32[4,8,1024]{2,1,0:T(8,128)S(1)}, f32[4,8,1024]{2,1,0:T(8,128)S(1)}, u32[]{:S(2)}, u32[]{:S(2)}) collective-permute-start(f32[4,8,1024]{2,1,0:T(8,128)S(1)} %get-tuple-element.114), channel_id=1, source_target_pairs={{0,8},{8,16},{16,24},{24,32},{32,40},{40,48},{48,56},{56,0},{1,9},... | collective-permute-start | bytes 393224 | tf_op jit(solution)/shard_map/ppermute | solution.py:417
  109.7 10.4 %collective-permute-start.7 = (f32[4,8,1024]{2,1,0:T(8,128)S(1)}, f32[4,8,1024]{2,1,0:T(8,128)S(1)}, u32[]{:S(2)}, u32[]{:S(2)}) collective-permute-start(f32[4,8,1024]{2,1,0:T(8,128)S(1)} %get-tuple-element.115), channel_id=1, source_target_pairs={{0,56},{8,0},{16,8},{24,16},{32,24},{40,32},{48,40},{56,48},{1,57}... | collective-permute-start | bytes 393224 | tf_op jit(solution)/shard_map/ppermute | solution.py:417
  120.1 13.1 %copy-start.19 = (f32[4,8,1024]{2,1,0:T(8,128)S(1)}, f32[4,8,1024]{2,1,0:T(8,128)}, u32[]{:S(2)}) copy-start(f32[4,8,1024]{2,1,0:T(8,128)} %get-tuple-element.136) | copy-start | bytes 393220
  120.2 14.7 %copy-start.17 = (f32[4,8,1024]{2,1,0:T(8,128)S(1)}, f32[4,8,1024]{2,1,0:T(8,128)}, u32[]{:S(2)}) copy-start(f32[4,8,1024]{2,1,0:T(8,128)} %get-tuple-element.133) | copy-start | bytes 393220
  120.2 16.7 %copy-start.18 = (f32[4,8,1024]{2,1,0:T(8,128)S(1)}, f32[4,8,1024]{2,1,0:T(8,128)}, u32[]{:S(2)}) copy-start(f32[4,8,1024]{2,1,0:T(8,128)} %get-tuple-element.140) | copy-start | bytes 393220
  120.2 17.9 %copy-start.16 = (f32[4,8,1024]{2,1,0:T(8,128)S(1)}, f32[4,8,1024]{2,1,0:T(8,128)}, u32[]{:S(2)}) copy-start(f32[4,8,1024]{2,1,0:T(8,128)} %get-tuple-element.144) | copy-start | bytes 393220
  120.8 36.7 %all-to-all-start.7 = ((f32[32,32,512]{2,1,0:T(8,128)}), f32[32,32,512]{2,1,0:T(8,128)S(1)}, u32[]{:S(2)}, u32[]{:S(2)}) async-start(f32[32,32,512]{2,1,0:T(8,128)} %get-tuple-element.128), calls=%async_computation.7 | async-start | bytes 4194304 | tf_op jit(solution)/shard_map/all_to_all | solution.py:421
  126.0 15.0 %copy-start.15 = (f32[4,8,1024]{2,1,0:T(8,128)S(1)}, f32[4,8,1024]{2,1,0:T(8,128)}, u32[]{:S(2)}) copy-start(f32[4,8,1024]{2,1,0:T(8,128)} %get-tuple-element.137) | copy-start | bytes 393220
  126.0 16.4 %copy-start.13 = (f32[4,8,1024]{2,1,0:T(8,128)S(1)}, f32[4,8,1024]{2,1,0:T(8,128)}, u32[]{:S(2)}) copy-start(f32[4,8,1024]{2,1,0:T(8,128)} %get-tuple-element.134) | copy-start | bytes 393220
  126.0 18.0 %copy-start.14 = (f32[4,8,1024]{2,1,0:T(8,128)S(1)}, f32[4,8,1024]{2,1,0:T(8,128)}, u32[]{:S(2)}) copy-start(f32[4,8,1024]{2,1,0:T(8,128)} %get-tuple-element.141) | copy-start | bytes 393220
  126.0 18.6 %copy-start.12 = (f32[4,8,1024]{2,1,0:T(8,128)S(1)}, f32[4,8,1024]{2,1,0:T(8,128)}, u32[]{:S(2)}) copy-start(f32[4,8,1024]{2,1,0:T(8,128)} %get-tuple-element.145) | copy-start | bytes 393220
  126.0 25.1 %copy-start.5 = (f32[4,8,1024]{2,1,0:T(8,128)S(1)}, f32[4,8,1024]{2,1,0:T(8,128)}, u32[]{:S(2)}) copy-start(f32[4,8,1024]{2,1,0:T(8,128)} %get-tuple-element.130.p0) | copy-start | bytes 393220
  126.0 25.0 %copy-start.6 = (f32[4,8,1024]{2,1,0:T(8,128)S(1)}, f32[4,8,1024]{2,1,0:T(8,128)}, u32[]{:S(2)}) copy-start(f32[4,8,1024]{2,1,0:T(8,128)} %get-tuple-element.138.p1) | copy-start | bytes 393220
  126.0 5.6 %collective-permute-start.16 = (f32[4,8,1024]{2,1,0:T(8,128)S(1)}, f32[4,8,1024]{2,1,0:T(8,128)S(1)}, u32[]{:S(2)}, u32[]{:S(2)}) collective-permute-start(f32[4,8,1024]{2,1,0:T(8,128)S(1)} %get-tuple-element.142), channel_id=1, source_target_pairs={{0,56},{8,0},{16,8},{24,16},{32,24},{40,32},{48,40},{56,48},{1,57}... | collective-permute-start | bytes 393224 | tf_op jit(solution)/shard_map/ppermute | solution.py:417
  127.2 7.6 %collective-permute-start.8 = (f32[4,8,1024]{2,1,0:T(8,128)S(1)}, f32[4,8,1024]{2,1,0:T(8,128)S(1)}, u32[]{:S(2)}, u32[]{:S(2)}) collective-permute-start(f32[4,8,1024]{2,1,0:T(8,128)S(1)} %add.32), channel_id=1, source_target_pairs={{0,8},{8,16},{16,24},{24,32},{32,40},{40,48},{48,56},{56,0},{1,9},... | collective-permute-start | bytes 393224 | tf_op jit(solution)/shard_map/ppermute | solution.py:417
  129.1 7.7 %collective-permute-start.13 = (f32[4,8,1024]{2,1,0:T(8,128)S(1)}, f32[4,8,1024]{2,1,0:T(8,128)S(1)}, u32[]{:S(2)}, u32[]{:S(2)}) collective-permute-start(f32[4,8,1024]{2,1,0:T(8,128)S(1)} %get-tuple-element.139), channel_id=1, source_target_pairs={{0,8},{8,16},{16,24},{24,32},{32,40},{40,48},{48,56},{56,0},{1,9},... | collective-permute-start | bytes 393224 | tf_op jit(solution)/shard_map/ppermute | solution.py:417
  131.7 6.4 %collective-permute-start.17 = (f32[4,8,1024]{2,1,0:T(8,128)S(1)}, f32[4,8,1024]{2,1,0:T(8,128)S(1)}, u32[]{:S(2)}, u32[]{:S(2)}) collective-permute-start(f32[4,8,1024]{2,1,0:T(8,128)S(1)} %add.39), channel_id=1, source_target_pairs={{0,56},{8,0},{16,8},{24,16},{32,24},{40,32},{48,40},{56,48},{1,57}... | collective-permute-start | bytes 393224 | tf_op jit(solution)/shard_map/ppermute | solution.py:417
  133.3 7.7 %collective-permute-start.11 = (f32[4,8,1024]{2,1,0:T(8,128)S(1)}, f32[4,8,1024]{2,1,0:T(8,128)S(1)}, u32[]{:S(2)}, u32[]{:S(2)}) collective-permute-start(f32[4,8,1024]{2,1,0:T(8,128)S(1)} %add.35), channel_id=1, source_target_pairs={{0,56},{8,0},{16,8},{24,16},{32,24},{40,32},{48,40},{56,48},{1,57}... | collective-permute-start | bytes 393224 | tf_op jit(solution)/shard_map/ppermute | solution.py:417
  134.9 7.5 %collective-permute-start.9 = (f32[4,8,1024]{2,1,0:T(8,128)S(1)}, f32[4,8,1024]{2,1,0:T(8,128)S(1)}, u32[]{:S(2)}, u32[]{:S(2)}) collective-permute-start(f32[4,8,1024]{2,1,0:T(8,128)S(1)} %add.33), channel_id=1, source_target_pairs={{0,8},{8,16},{16,24},{24,32},{32,40},{40,48},{48,56},{56,0},{1,9},... | collective-permute-start | bytes 393224 | tf_op jit(solution)/shard_map/ppermute | solution.py:417
  136.9 7.0 %collective-permute-start.14 = (f32[4,8,1024]{2,1,0:T(8,128)S(1)}, f32[4,8,1024]{2,1,0:T(8,128)S(1)}, u32[]{:S(2)}, u32[]{:S(2)}) collective-permute-start(f32[4,8,1024]{2,1,0:T(8,128)S(1)} %add.37), channel_id=1, source_target_pairs={{0,8},{8,16},{16,24},{24,32},{32,40},{40,48},{48,56},{56,0},{1,9},... | collective-permute-start | bytes 393224 | tf_op jit(solution)/shard_map/ppermute | solution.py:417
  138.1 6.4 %collective-permute-start.18 = (f32[4,8,1024]{2,1,0:T(8,128)S(1)}, f32[4,8,1024]{2,1,0:T(8,128)S(1)}, u32[]{:S(2)}, u32[]{:S(2)}) collective-permute-start(f32[4,8,1024]{2,1,0:T(8,128)S(1)} %add.40), channel_id=1, source_target_pairs={{0,56},{8,0},{16,8},{24,16},{32,24},{40,32},{48,40},{56,48},{1,57}... | collective-permute-start | bytes 393224 | tf_op jit(solution)/shard_map/ppermute | solution.py:417
  141.0 6.9 %collective-permute-start.12 = (f32[4,8,1024]{2,1,0:T(8,128)S(1)}, f32[4,8,1024]{2,1,0:T(8,128)S(1)}, u32[]{:S(2)}, u32[]{:S(2)}) collective-permute-start(f32[4,8,1024]{2,1,0:T(8,128)S(1)} %add.36), channel_id=1, source_target_pairs={{0,56},{8,0},{16,8},{24,16},{32,24},{40,32},{48,40},{56,48},{1,57}... | collective-permute-start | bytes 393224 | tf_op jit(solution)/shard_map/ppermute | solution.py:417
  142.4 7.2 %collective-permute-start.10 = (f32[4,8,1024]{2,1,0:T(8,128)S(1)}, f32[4,8,1024]{2,1,0:T(8,128)S(1)}, u32[]{:S(2)}, u32[]{:S(2)}) collective-permute-start(f32[4,8,1024]{2,1,0:T(8,128)S(1)} %add.34), channel_id=1, source_target_pairs={{0,8},{8,16},{16,24},{24,32},{32,40},{40,48},{48,56},{56,0},{1,9},... | collective-permute-start | bytes 393224 | tf_op jit(solution)/shard_map/ppermute | solution.py:417
  143.9 13.5 %copy-start.3 = (f32[40,480]{1,0:T(8,128)S(1)}, f32[40,480]{1,0:T(8,128)}, u32[]{:S(2)}) copy-start(f32[40,480]{1,0:T(8,128)} %get-tuple-element.129.mine) | copy-start | bytes 230404
  144.0 7.1 %collective-permute-start.15 = (f32[4,8,1024]{2,1,0:T(8,128)S(1)}, f32[4,8,1024]{2,1,0:T(8,128)S(1)}, u32[]{:S(2)}, u32[]{:S(2)}) collective-permute-start(f32[4,8,1024]{2,1,0:T(8,128)S(1)} %add.38), channel_id=1, source_target_pairs={{0,8},{8,16},{16,24},{24,32},{32,40},{40,48},{48,56},{56,0},{1,9},... | collective-permute-start | bytes 393224 | tf_op jit(solution)/shard_map/ppermute | solution.py:417
  144.6 6.5 %collective-permute-start.19 = (f32[4,8,1024]{2,1,0:T(8,128)S(1)}, f32[4,8,1024]{2,1,0:T(8,128)S(1)}, u32[]{:S(2)}, u32[]{:S(2)}) collective-permute-start(f32[4,8,1024]{2,1,0:T(8,128)S(1)} %add.41), channel_id=1, source_target_pairs={{0,56},{8,0},{16,8},{24,16},{32,24},{40,32},{48,40},{56,48},{1,57}... | collective-permute-start | bytes 393224 | tf_op jit(solution)/shard_map/ppermute | solution.py:417
  151.6 6.5 %collective-permute-start.20 = (f32[8,2048]{1,0:T(8,128)S(1)}, f32[8,2048]{1,0:T(8,128)S(1)}, u32[]{:S(2)}, u32[]{:S(2)}) collective-permute-start(f32[8,2048]{1,0:T(8,128)S(1)} %get-tuple-element.146), channel_id=1, source_target_pairs={{0,64},{64,128},{128,192},{192,0},{1,65},{65,129},{129,193},{193,1... | collective-permute-start | bytes 196616 | tf_op jit(solution)/shard_map/ppermute | solution.py:417
  153.2 5.8 %collective-permute-start.21 = (f32[8,2048]{1,0:T(8,128)S(1)}, f32[8,2048]{1,0:T(8,128)S(1)}, u32[]{:S(2)}, u32[]{:S(2)}) collective-permute-start(f32[8,2048]{1,0:T(8,128)S(1)} %get-tuple-element.147), channel_id=1, source_target_pairs={{0,128},{64,192},{128,0},{192,64},{1,129},{65,193},{129,1},{193,65... | collective-permute-start | bytes 196616 | tf_op jit(solution)/shard_map/ppermute | solution.py:417
  156.0 4.3 %collective-permute-start.22 = (f32[8,2048]{1,0:T(8,128)S(1)}, f32[8,2048]{1,0:T(8,128)S(1)}, u32[]{:S(2)}, u32[]{:S(2)}) collective-permute-start(f32[8,2048]{1,0:T(8,128)S(1)} %get-tuple-element.148), channel_id=1, source_target_pairs={{0,192},{64,0},{128,64},{192,128},{1,193},{65,1},{129,65},{193,129... | collective-permute-start | bytes 196616 | tf_op jit(solution)/shard_map/ppermute | solution.py:417
  (11 other events, 66.6 us)
